TPU v7x, 128 devices: a whole 4x4x4 slice. The times are simulated.
128 devices in a mesh: gx: 16 (over y_hi, x, core), gy: 8 (over y_lo, z).
Axes of the slice: x: 4, y: 4 (y_hi: 2, y_lo: 2; y = y_hi * 2 + y_lo), z: 4, core: 2. Of those that a mesh axis runs over, the one named last changes fastest.
Arguments:
- air_vector: float32 [128, 256, 2048], P(None, 'gx', 'gy'), may hold values from -6 to 6
- sea_vector: float32 [64, 128, 4096], P(None, 'gx', 'gy'), may hold values from -6 to 6
- air_scaling: float32 [128, 256, 2048], P(None, 'gx', 'gy'), may hold values from 0.5 to 2
- sea_scaling: float32 [64, 128, 4096], P(None, 'gx', 'gy'), may hold values from 0.5 to 2
- air_weights: float32 [128, 256, 2048], P(None, 'gx', 'gy'), may hold values from 0.3 to 3
- sea_weights: float32 [64, 128, 4096], P(None, 'gx', 'gy'), may hold values from 0.3 to 3
- air_column: float32 [128, 128], replicated, may hold values from -0.5 to 0.5
- sea_column: float32 [64, 64], replicated, may hold values from -0.75 to 0.75
- land_mask: int32 [128, 4096], P('gx', 'gy'), may hold values 0 or 1
- flux_index: int32 [8, 512, 4], P('gy', 'gx'), may hold values from 0 to 511, as said below
- flux_count: int32 [8, 512], P('gy', 'gx'), may hold values from 1 to 4
- flux_tiles: bfloat16 [8, 512, 4, 128, 128], P('gy', 'gx'), may hold values from -0.25 to 0.25
- skin_index: int32 [8, 512, 4], P('gy', 'gx'), may hold values from 0 to 511, as said below
- skin_count: int32 [8, 512], P('gy', 'gx'), may hold values from 1 to 4
- skin_tiles: bfloat16 [8, 512, 4, 128, 128], P('gy', 'gx'), may hold values from -0.25 to 0.25
Outputs:
- air_gradient: float32 [128, 256, 2048], P(None, 'gx', 'gy')
- sea_gradient: float32 [64, 128, 4096], P(None, 'gx', 'gy')
Inputs may be any that keep to these rules, and one draw needn't show every extreme that they name: `flux_index`: slot 0 names the atmosphere block with the same number as the ocean block; every other slot names that block or one beside it in the tile row (block 511 lies beside block 0); slots at or past the count are padding and are not used. `skin_index`: slot 0 names the ocean block with the same number as the atmosphere block; every other slot names that block or one beside it in the tile row (block 511 lies beside block 0); slots at or past the count are padding and are not used.
All inputs are finite; a program needn't handle non-finite values. No bound on the sum of `land_mask` on one device may be relied on, other than what follows from the above.
Results may differ from a plain program's by a relative error of at most 0.00069.
Values may be sent and summed in bfloat16 or wider, within the bound.
A program may use at most 128 MiB of HBM per device.

v0:
```python
import jax
import jax.numpy as jnp
from jax import lax
from jax.sharding import PartitionSpec as P

FIELDS = 4


lap_gain = 0.2


def extended(cells, sides, width, closed):
    for axis, dim in sides:
        count = lax.axis_size(axis)
        ends = count if closed else count - 1
        head = lax.slice_in_dim(cells, 0, width, axis=dim)
        tail = lax.slice_in_dim(cells, cells.shape[dim] - width, cells.shape[dim], axis=dim)
        cells = jnp.concatenate(
            [
                lax.ppermute(tail, axis, [(i, (i + 1) % count) for i in range(ends)]),
                cells,
                lax.ppermute(head, axis, [((i + 1) % count, i) for i in range(ends)]),
            ],
            axis=dim,
        )
    return cells


def shifted(shard, axis, by):
    devices = lax.axis_size(axis)
    return lax.ppermute(shard, axis, [(i, (i + by) % devices) for i in range(devices)])


def laplace(grid_field):
    padded_x = extended(grid_field, (("gx", 1),), 1, True)
    padded_y = extended(grid_field, (("gy", 2),), 1, False)
    east_west = padded_x[:, 2:, :] + padded_x[:, :-2, :]
    north_south = padded_y[:, :, 2:] + padded_y[:, :, :-2]
    return east_west + north_south - 4.0 * grid_field


def columns(matrix, grid_field):
    levels = grid_field.shape[0]
    flat_field = grid_field.reshape(levels, -1)
    product = jnp.dot(
        matrix, flat_field, precision=lax.Precision.HIGHEST, preferred_element_type=jnp.float32
    )
    return product.reshape(grid_field.shape)


def slot_mask(slot_count, slots):
    return jnp.arange(slots)[None, :] < slot_count[:, None]


def local_places(slot_index, rows_here):
    row_length = rows_here * lax.axis_size("gx")
    my_first = lax.axis_index("gx") * rows_here
    return jnp.mod(slot_index - my_first + 1, row_length)


def regrid_forward(rimmed_blocks, slot_index, slot_count, slot_tiles):
    rows_here = rimmed_blocks.shape[1] - 2
    places = local_places(slot_index, rows_here)
    picked = jnp.take(rimmed_blocks, places, axis=1)
    in_use = slot_mask(slot_count, slot_index.shape[1])
    picked = jnp.where(in_use[None, :, :, None], picked, jnp.zeros((), jnp.bfloat16))
    return jnp.einsum("okij,fokj->foi", slot_tiles, picked, preferred_element_type=jnp.float32)


def back_terms(adjoint_blocks, slot_index, slot_count, slot_tiles):
    rows_here = adjoint_blocks.shape[1]
    contributions = jnp.einsum(
        "okij,foi->okfj", slot_tiles, adjoint_blocks, preferred_element_type=jnp.float32
    )
    in_use = slot_mask(slot_count, slot_index.shape[1])
    contributions = jnp.where(in_use[:, :, None, None], contributions, jnp.zeros((), jnp.float32))
    fields = contributions.shape[2]
    block = contributions.shape[3]
    flat_terms = contributions.reshape(-1, fields, block)
    places = local_places(slot_index, rows_here).reshape(-1)
    onehot = (places[:, None] == jnp.arange(rows_here + 2)[None, :]).astype(jnp.float32)
    return jnp.einsum("mfb,mr->rfb", flat_terms, onehot, precision=lax.Precision.HIGHEST)


def shards(
    air_vector,
    sea_vector,
    air_scaling,
    sea_scaling,
    air_weights,
    sea_weights,
    air_column,
    sea_column,
    land_mask,
    flux_index,
    flux_count,
    flux_tiles,
    skin_index,
    skin_count,
    skin_tiles,
):
    air_levels = air_vector.shape[0]
    block = flux_tiles.shape[-1]
    air_shape = (FIELDS,) + air_vector.shape[1:]
    sea_shape = (FIELDS,) + sea_vector.shape[1:]
    sea_mask = land_mask.astype(jnp.float32)[None]
    low_first = air_levels - FIELDS
    air_one = air_vector + lap_gain * laplace(air_vector)
    air_two = columns(air_column, air_scaling * air_one)
    sea_zero = sea_mask * sea_vector
    sea_one = sea_zero + lap_gain * sea_mask * laplace(sea_zero)
    air_surface = air_two[low_first:].astype(jnp.bfloat16).reshape(FIELDS, -1, block)
    sea_surface = sea_one[:FIELDS].astype(jnp.bfloat16).reshape(FIELDS, -1, block)
    surfaces = jnp.stack([air_surface, sea_surface])
    rimmed = extended(surfaces, (("gx", 2),), 1, True)
    flux_sea = regrid_forward(rimmed[0], flux_index[0], flux_count[0], flux_tiles[0]).reshape(
        sea_shape
    )
    skin_air = regrid_forward(rimmed[1], skin_index[0], skin_count[0], skin_tiles[0]).reshape(
        air_shape
    )
    sea_two = sea_one.at[:FIELDS].add(sea_mask * flux_sea)
    sea_three = sea_mask * columns(sea_column, sea_scaling * sea_two)
    air_three = air_two.at[low_first:].add(skin_air)
    air_forcing = air_weights * air_three
    sea_forcing = sea_weights * sea_three
    sea_adjoint = sea_scaling * columns(sea_column.T, sea_mask * sea_forcing)
    flux_adjoint = (sea_mask * sea_adjoint[:FIELDS]).astype(jnp.bfloat16).reshape(FIELDS, -1, block)
    skin_adjoint = air_forcing[low_first:].astype(jnp.bfloat16).reshape(FIELDS, -1, block)
    flux_dense = back_terms(flux_adjoint, flux_index[0], flux_count[0], flux_tiles[0])
    skin_dense = back_terms(skin_adjoint, skin_index[0], skin_count[0], skin_tiles[0])
    both_dense = jnp.stack([flux_dense, skin_dense])
    from_left = shifted(both_dense[:, -1], "gx", 1)
    from_right = shifted(both_dense[:, 0], "gx", -1)
    kept = both_dense[:, 1:-1]
    kept = kept.at[:, 0].add(from_left)
    kept = kept.at[:, -1].add(from_right)
    flux_back = kept[0].transpose(1, 0, 2).reshape(air_shape)
    skin_back = kept[1].transpose(1, 0, 2).reshape(sea_shape)
    sea_upper = sea_adjoint.at[:FIELDS].add(skin_back)
    sea_gradient = sea_mask * (sea_upper + lap_gain * laplace(sea_mask * sea_upper))
    air_lower = air_forcing.at[low_first:].add(flux_back)
    air_upper = air_scaling * columns(air_column.T, air_lower)
    air_gradient = air_upper + lap_gain * laplace(air_upper)
    return (air_gradient, sea_gradient)


def solution(mesh):
    return jax.shard_map(
        shards,
        mesh=mesh,
        in_specs=(
            P(None, "gx", "gy"),
            P(None, "gx", "gy"),
            P(None, "gx", "gy"),
            P(None, "gx", "gy"),
            P(None, "gx", "gy"),
            P(None, "gx", "gy"),
            P(),
            P(),
            P("gx", "gy"),
            P("gy", "gx", None),
            P("gy", "gx"),
            P("gy", "gx", None, None, None),
            P("gy", "gx", None),
            P("gy", "gx"),
            P("gy", "gx", None, None, None),
        ),
        out_specs=(P(None, "gx", "gy"), P(None, "gx", "gy")),
        check_vma=False,
    )
```

profile of v0, /device:TPU:96, one launch (start us, length us, event | category | flops | bytes accessed | tf_op | source)
XLA Modules:
  0.0 157.9 jit_solution(12692815295640602013)
XLA Ops:
  3.7 2.3 %collective-permute-start.6 = (f32[64,8,1]{2,1,0:T(8,128)}, f32[64,8,1]{2,1,0:T(8,128)}, u32[]{:S(2)}, u32[]{:S(2)}) collective-permute-start(f32[64,8,1]{2,1,0:T(8,128)} %get-tuple-element.101), channel_id=1, source_target_pairs={{1,0},{2,1},{3,2},{4,3},{5,4},{6,5},{7,6},{9,8},{10,9},{11,10},{12... | collective-permute-start | bytes 6152 | tf_op jit(solution)/shard_map/ppermute | solution.py:22
  6.0 5.6 %collective-permute-start.7 = (f32[64,8,1]{2,1,0:T(8,128)}, f32[64,8,1]{2,1,0:T(8,128)}, u32[]{:S(2)}, u32[]{:S(2)}) collective-permute-start(f32[64,8,1]{2,1,0:T(8,128)} %get-tuple-element.102), channel_id=1, source_target_pairs={{0,1},{1,2},{2,3},{3,4},{4,5},{5,6},{6,7},{8,9},{9,10},{10,11},{11... | collective-permute-start | bytes 6152 | tf_op jit(solution)/shard_map/ppermute | solution.py:20
  12.5 4.3 %collective-permute-start.4 = (f32[64,1,512]{2,1,0:T(1,128)}, f32[64,1,512]{2,1,0:T(1,128)}, u32[]{:S(2)}, u32[]{:S(2)}) collective-permute-start(f32[64,1,512]{2,1,0:T(1,128)} %get-tuple-element.99), channel_id=1, source_target_pairs={{8,0},{16,8},{24,16},{32,24},{40,32},{48,40},{56,48},{64,56},{72,6... | collective-permute-start | bytes 393224 | tf_op jit(solution)/shard_map/ppermute | solution.py:22
  30.3 2.2 %copy.206 = f32[128,16,1]{0,1,2:T(8,128)} copy(f32[128,16,1]{2,1,0:T(8,128)} %get-tuple-element.94) | data formatting | bytes 16384
  35.5 6.0 %collective-permute-start.3 = (f32[128,16,1]{0,1,2:T(8,128)}, f32[128,16,1]{0,1,2:T(8,128)}, u32[]{:S(2)}, u32[]{:S(2)}) collective-permute-start(f32[128,16,1]{0,1,2:T(8,128)} %copy.206), channel_id=1, source_target_pairs={{0,1},{1,2},{2,3},{3,4},{4,5},{5,6},{6,7},{8,9},{9,10},{10,11},{11... | collective-permute-start | bytes 24584 | tf_op jit(solution)/shard_map/ppermute | solution.py:20
  41.5 4.8 %collective-permute-start = (f32[128,1,256]{2,0,1:T(8,128)}, f32[128,1,256]{2,0,1:T(8,128)}, u32[]{:S(2)}, u32[]{:S(2)}) collective-permute-start(f32[128,1,256]{2,0,1:T(8,128)} %copy.203), channel_id=1, source_target_pairs={{8,0},{16,8},{24,16},{32,24},{40,32},{48,40},{56,48},{64,56},{72,6... | collective-permute-start | bytes 393224 | tf_op jit(solution)/shard_map/ppermute | solution.py:22
  50.3 4.1 %collective-permute-done.1 = f32[128,1,256]{2,0,1:T(8,128)} collective-permute-done((f32[128,1,256]{2,0,1:T(8,128)S(1)}, f32[128,1,256]{2,0,1:T(8,128)}, u32[]{:S(2)}, u32[]{:S(2)}) %collective-permute-start.1) | collective-permute-done | bytes 131104 | tf_op jit(solution)/shard_map/ppermute | solution.py:20
  55.5 5.3 %fusion.19 = f32[128,16,256]{0,2,1:T(8,128)S(1)} fusion(f32[128,16,256]{0,2,1:T(8,128)S(1)} %copy.184, f32[128,16,256]{0,2,1:T(8,128)} %copy.162, f32[128,16,1]{0,2,1:T(1,128)} %bitcast.1, f32[128,16,1]{0,2,1:T(1,128)S(1)} %bitcast.152, f32[128,1,256]{0,2,1:T(8,128)S(1)} %copy.153, f32[128,1,256]{0,2,1:T(8,128)S(1)} %copy.151), kind=kLoop, calls=%fused_computation.26 | loop fusion | flops 6291456 | bytes 6569984 | tf_op jit(solution)/shard_map/mul | solution.py:109
  63.5 5.3 %collective-permute-start.9 = (bf16[2,4,1,128]{3,1,2,0:T(4,128)(2,1)S(1)}, bf16[2,4,1,128]{3,1,2,0:T(4,128)(2,1)S(1)}, u32[]{:S(2)}, u32[]{:S(2)}) collective-permute-start(bf16[2,4,1,128]{3,1,2,0:T(4,128)(2,1)S(1)} %get-tuple-element.111), channel_id=1, source_target_pairs={{8,0},{16,8},{24,16},{32,24},{40,32},{48,40},{56,48},{64,56},{72,6... | collective-permute-start | bytes 6152 | tf_op jit(solution)/shard_map/ppermute | solution.py:22
  71.0 2.2 %copy.169 = f32[4,16,256]{2,1,0:T(8,128)S(1)} copy(f32[4,16,256]{0,2,1:T(8,128)} %bitcast.137) | data formatting | bytes 131072 | tf_op jit(solution)/shard_map/reshape.322
  76.2 3.2 %fusion.30 = f32[4,32,128]{2,0,1:T(4,128)S(1)} fusion(bf16[1,32,4,128,128]{4,3,2,1,0:T(8,128)(2,1)} %param.40, bf16[32,4,4,128]{3,2,1,0:T(4,128)(2,1)S(1)} %bitcast.149, pred[32,4]{1,0:T(8,128)(4,1)S(1)} %copy.172, pred[32,4]{1,0:T(8,128)(4,1)S(1)} %iota_compare_fusion.2), kind=kOutput, calls=%fused_computation.36 | convolution fusion | flops 16908288 | bytes 4391168 | tf_op jit(solution)/shard_map/okij,fokj->foi/dot_general | solution.py:67
  84.8 2.9 %fusion.24 = f32[32,4,4,128]{3,1,2,0:T(4,128)S(1)} fusion(bf16[1,32,4,128,128]{4,3,2,1,0:T(8,128)(2,1)} %param.40, pred[32,4]{1,0:T(8,128)(4,1)S(1)} %iota_compare_fusion.2, bf16[4,32,128,1]{2,1,0,3:T(8,128)(2,1)S(1)} %bitcast.147), kind=kOutput, calls=%fused_computation.32 | convolution fusion | flops 16842752 | bytes 4489344 | tf_op jit(solution)/shard_map/okij,foi->okfj/dot_general | solution.py:72
  88.4 3.0 %fusion.27 = f32[4,32,128]{2,0,1:T(4,128)S(1)} fusion(bf16[1,32,4,128,128]{4,3,2,1,0:T(8,128)(2,1)} %param.43, bf16[32,4,4,128]{3,2,1,0:T(4,128)(2,1)S(1)} %bitcast.150, pred[32,4]{1,0:T(8,128)(4,1)S(1)} %copy.164, pred[32,4]{1,0:T(8,128)(4,1)S(1)} %iota_compare_fusion.3), kind=kOutput, calls=%fused_computation.35 | convolution fusion | flops 16908288 | bytes 4391168 | tf_op jit(solution)/shard_map/okij,fokj->foi/dot_general | solution.py:67
  92.1 2.7 %mul.120 = f32[128,16,256]{2,1,0:T(8,128)S(1)} multiply(f32[128,16,256]{2,1,0:T(8,128)} %param.33, f32[128,16,256]{2,1,0:T(8,128)} %add_dynamic-update-slice_fusion.3) | non-fusion elementwise | flops 524288 | bytes 6291456 | tf_op jit(solution)/shard_map/mul | solution.py:125
  94.9 2.8 %fusion.21 = f32[32,4,4,128]{3,1,2,0:T(4,128)S(1)} fusion(bf16[1,32,4,128,128]{4,3,2,1,0:T(8,128)(2,1)} %param.43, pred[32,4]{1,0:T(8,128)(4,1)} %copy-done.13, bf16[4,32,128,1]{2,1,0,3:T(8,128)(2,1)S(1)} %bitcast.148), kind=kOutput, calls=%fused_computation.31 | convolution fusion | flops 16842752 | bytes 4489344 | tf_op jit(solution)/shard_map/okij,foi->okfj/dot_general | solution.py:72
  98.5 5.6 %collective-permute-start.11 = (f32[2,4,128]{2,1,0:T(4,128)S(1)}, f32[2,4,128]{2,1,0:T(4,128)S(1)}, u32[]{:S(2)}, u32[]{:S(2)}) collective-permute-start(f32[2,4,128]{2,1,0:T(4,128)S(1)} %bitcast.157), channel_id=1, source_target_pairs={{0,120},{8,0},{16,8},{24,16},{32,24},{40,32},{48,40},{56,48},{64,5... | collective-permute-start | bytes 12296 | tf_op jit(solution)/shard_map/ppermute | solution.py:31
  107.2 3.5 %fusion.92 = f32[4096,128]{1,0:T(8,128)S(1)} fusion(f32[128,4096]{1,0:T(8,128)S(1)} %bitcast.136, f32[128,128]{1,0:T(8,128)S(1)} %copy-done), kind=kOutput, calls=%fused_computation.157 | convolution fusion | flops 805306368 | bytes 4259840 | tf_op jit(solution)/shard_map/dot_general | solution.py:45
  115.8 5.3 %collective-permute-start.12 = (f32[128,1,256]{2,0,1:T(8,128)}, f32[128,1,256]{2,0,1:T(8,128)}, u32[]{:S(2)}, u32[]{:S(2)}) collective-permute-start(f32[128,1,256]{2,0,1:T(8,128)} %copy.185), channel_id=1, source_target_pairs={{8,0},{16,8},{24,16},{32,24},{40,32},{48,40},{56,48},{64,56},{72,6... | collective-permute-start | bytes 393224 | tf_op jit(solution)/shard_map/ppermute | solution.py:22
  123.8 6.0 %collective-permute-start.15 = (f32[128,16,1]{0,1,2:T(8,128)S(1)}, f32[128,16,1]{0,1,2:T(8,128)S(1)}, u32[]{:S(2)}, u32[]{:S(2)}) collective-permute-start(f32[128,16,1]{0,1,2:T(8,128)S(1)} %bitcast.155), channel_id=1, source_target_pairs={{0,1},{1,2},{2,3},{3,4},{4,5},{5,6},{6,7},{8,9},{9,10},{10,11},{11... | collective-permute-start | bytes 24584 | tf_op jit(solution)/shard_map/ppermute | solution.py:20
  133.7 6.0 %collective-permute-start.19 = (f32[64,8,1]{2,1,0:T(8,128)}, f32[64,8,1]{2,1,0:T(8,128)}, u32[]{:S(2)}, u32[]{:S(2)}) collective-permute-start(f32[64,8,1]{2,1,0:T(8,128)} %get-tuple-element.98), channel_id=1, source_target_pairs={{0,1},{1,2},{2,3},{3,4},{4,5},{5,6},{6,7},{8,9},{9,10},{10,11},{11... | collective-permute-start | bytes 6152 | tf_op jit(solution)/shard_map/ppermute | solution.py:20
  141.4 4.2 %collective-permute-start.16 = (f32[64,1,512]{2,1,0:T(1,128)}, f32[64,1,512]{2,1,0:T(1,128)}, u32[]{:S(2)}, u32[]{:S(2)}) collective-permute-start(f32[64,1,512]{2,1,0:T(1,128)} %get-tuple-element.95), channel_id=1, source_target_pairs={{8,0},{16,8},{24,16},{32,24},{40,32},{48,40},{56,48},{64,56},{72,6... | collective-permute-start | bytes 393224 | tf_op jit(solution)/shard_map/ppermute | solution.py:22
  148.8 3.1 %copy.194 = f32[128,16,256]{2,1,0:T(8,128)} copy(f32[128,16,256]{0,2,1:T(8,128)} %fusion.12) | data formatting | bytes 4194304
  151.9 3.1 %collective-permute-done.17 = f32[64,1,512]{2,1,0:T(1,128)} collective-permute-done((f32[64,1,512]{2,1,0:T(1,128)}, f32[64,1,512]{2,1,0:T(1,128)}, u32[]{:S(2)}, u32[]{:S(2)}) %collective-permute-start.17) | collective-permute-done | bytes 131104 | tf_op jit(solution)/shard_map/ppermute | solution.py:20
  155.0 2.9 %fusion.40 = f32[64,8,512]{2,1,0:T(8,128)} fusion(f32[64,8,512]{2,1,0:T(8,128)S(1)} %add_dynamic-update-slice_fusion, f32[64,8,512]{2,1,0:T(8,128)S(1)} %copy-done.5, f32[64,8,1]{2,1,0:T(8,128)} %collective-permute-done.19, f32[64,8,1]{2,1,0:T(8,128)} %collective-permute-done.18, f32[64,1,512]{2,1,0:T(1,128)} %collective-permute-done.17, ...), kind=kLoop, calls=%fused_computation.47 | loop fusion | flops 3145728 | bytes 3428352 | tf_op jit(solution)/shard_map/mul | solution.py:141
  (163 shorter events, 59.7 us)
Async XLA Ops:
  0.6 60.2 %copy-start = (f32[128,128]{1,0:T(8,128)S(1)}, f32[128,128]{1,0:T(8,128)}, u32[]{:S(2)}) copy-start(f32[128,128]{1,0:T(8,128)} %param.35) | copy-start | bytes 196612
  0.6 16.3 %copy-start.3 = (f32[128,16,256]{2,1,0:T(8,128)S(1)}, f32[128,16,256]{2,1,0:T(8,128)}, u32[]{:S(2)}) copy-start(f32[128,16,256]{2,1,0:T(8,128)} %param.29) | copy-start | bytes 6291460
  3.7 31.8 %collective-permute-start.6 = (f32[64,8,1]{2,1,0:T(8,128)}, f32[64,8,1]{2,1,0:T(8,128)}, u32[]{:S(2)}, u32[]{:S(2)}) collective-permute-start(f32[64,8,1]{2,1,0:T(8,128)} %get-tuple-element.101), channel_id=1, source_target_pairs={{1,0},{2,1},{3,2},{4,3},{5,4},{6,5},{7,6},{9,8},{10,9},{11,10},{12... | collective-permute-start | bytes 6152 | tf_op jit(solution)/shard_map/ppermute | solution.py:22
  6.0 35.5 %collective-permute-start.7 = (f32[64,8,1]{2,1,0:T(8,128)}, f32[64,8,1]{2,1,0:T(8,128)}, u32[]{:S(2)}, u32[]{:S(2)}) collective-permute-start(f32[64,8,1]{2,1,0:T(8,128)} %get-tuple-element.102), channel_id=1, source_target_pairs={{0,1},{1,2},{2,3},{3,4},{4,5},{5,6},{6,7},{8,9},{9,10},{10,11},{11... | collective-permute-start | bytes 6152 | tf_op jit(solution)/shard_map/ppermute | solution.py:20
  12.5 33.8 %collective-permute-start.4 = (f32[64,1,512]{2,1,0:T(1,128)}, f32[64,1,512]{2,1,0:T(1,128)}, u32[]{:S(2)}, u32[]{:S(2)}) collective-permute-start(f32[64,1,512]{2,1,0:T(1,128)} %get-tuple-element.99), channel_id=1, source_target_pairs={{8,0},{16,8},{24,16},{32,24},{40,32},{48,40},{56,48},{64,56},{72,6... | collective-permute-start | bytes 393224 | tf_op jit(solution)/shard_map/ppermute | solution.py:22
  16.8 29.6 %collective-permute-start.5 = (f32[64,1,512]{2,1,0:T(1,128)}, f32[64,1,512]{2,1,0:T(1,128)}, u32[]{:S(2)}, u32[]{:S(2)}) collective-permute-start(f32[64,1,512]{2,1,0:T(1,128)} %get-tuple-element.100), channel_id=1, source_target_pairs={{0,8},{8,16},{16,24},{24,32},{32,40},{40,48},{48,56},{56,64},{64,7... | collective-permute-start | bytes 393224 | tf_op jit(solution)/shard_map/ppermute | solution.py:20
  20.2 35.3 %collective-permute-start.2 = (f32[128,16,1]{0,1,2:T(8,128)S(1)}, f32[128,16,1]{0,1,2:T(8,128)S(1)}, u32[]{:S(2)}, u32[]{:S(2)}) collective-permute-start(f32[128,16,1]{0,1,2:T(8,128)S(1)} %copy.205), channel_id=1, source_target_pairs={{1,0},{2,1},{3,2},{4,3},{5,4},{6,5},{7,6},{9,8},{10,9},{11,10},{12... | collective-permute-start | bytes 24584 | tf_op jit(solution)/shard_map/ppermute | solution.py:22
  24.5 63.9 %copy-start.13 = (pred[32,4]{1,0:T(8,128)(4,1)}, pred[32,4]{1,0:T(8,128)(4,1)S(1)}, u32[]{:S(2)}) copy-start(pred[32,4]{1,0:T(8,128)(4,1)S(1)} %iota_compare_fusion.3) | copy-start | bytes 388
  34.5 26.3 %copy-start.1 = (f32[128,16,256]{0,2,1:T(8,128)}, f32[128,16,256]{0,2,1:T(8,128)S(1)}, u32[]{:S(2)}) copy-start(f32[128,16,256]{0,2,1:T(8,128)S(1)} %copy.184) | copy-start | bytes 6291460
  35.5 20.0 %collective-permute-start.3 = (f32[128,16,1]{0,1,2:T(8,128)}, f32[128,16,1]{0,1,2:T(8,128)}, u32[]{:S(2)}, u32[]{:S(2)}) collective-permute-start(f32[128,16,1]{0,1,2:T(8,128)} %copy.206), channel_id=1, source_target_pairs={{0,1},{1,2},{2,3},{3,4},{4,5},{5,6},{6,7},{8,9},{9,10},{10,11},{11... | collective-permute-start | bytes 24584 | tf_op jit(solution)/shard_map/ppermute | solution.py:20
  41.5 7.8 %collective-permute-start = (f32[128,1,256]{2,0,1:T(8,128)}, f32[128,1,256]{2,0,1:T(8,128)}, u32[]{:S(2)}, u32[]{:S(2)}) collective-permute-start(f32[128,1,256]{2,0,1:T(8,128)} %copy.203), channel_id=1, source_target_pairs={{8,0},{16,8},{24,16},{32,24},{40,32},{48,40},{56,48},{64,56},{72,6... | collective-permute-start | bytes 393224 | tf_op jit(solution)/shard_map/ppermute | solution.py:22
  46.4 8.1 %collective-permute-start.1 = (f32[128,1,256]{2,0,1:T(8,128)S(1)}, f32[128,1,256]{2,0,1:T(8,128)}, u32[]{:S(2)}, u32[]{:S(2)}) collective-permute-start(f32[128,1,256]{2,0,1:T(8,128)S(1)} %copy.204), channel_id=1, source_target_pairs={{0,8},{8,16},{16,24},{24,32},{32,40},{40,48},{48,56},{56,64},{64,7... | collective-permute-start | bytes 393224 | tf_op jit(solution)/shard_map/ppermute | solution.py:20
  63.4 11.9 %collective-permute-start.8 = (bf16[2,4,1,128]{3,1,2,0:T(4,128)(2,1)S(1)}, bf16[2,4,1,128]{3,1,2,0:T(4,128)(2,1)S(1)}, u32[]{:S(2)}, u32[]{:S(2)}) collective-permute-start(bf16[2,4,1,128]{3,1,2,0:T(4,128)(2,1)S(1)} %get-tuple-element.110), channel_id=1, source_target_pairs={{0,8},{8,16},{16,24},{24,32},{32,40},{40,48},{48,56},{56,64},{64,7... | collective-permute-start | bytes 6152 | tf_op jit(solution)/shard_map/ppermute | solution.py:20
  63.5 11.8 %collective-permute-start.9 = (bf16[2,4,1,128]{3,1,2,0:T(4,128)(2,1)S(1)}, bf16[2,4,1,128]{3,1,2,0:T(4,128)(2,1)S(1)}, u32[]{:S(2)}, u32[]{:S(2)}) collective-permute-start(bf16[2,4,1,128]{3,1,2,0:T(4,128)(2,1)S(1)} %get-tuple-element.111), channel_id=1, source_target_pairs={{8,0},{16,8},{24,16},{32,24},{40,32},{48,40},{56,48},{64,56},{72,6... | collective-permute-start | bytes 6152 | tf_op jit(solution)/shard_map/ppermute | solution.py:22
  98.3 6.7 %collective-permute-start.10 = (f32[2,4,128]{2,1,0:T(4,128)S(1)}, f32[2,4,128]{2,1,0:T(4,128)S(1)}, u32[]{:S(2)}, u32[]{:S(2)}) collective-permute-start(f32[2,4,128]{2,1,0:T(4,128)S(1)} %bitcast.158), channel_id=1, source_target_pairs={{0,8},{8,16},{16,24},{24,32},{32,40},{40,48},{48,56},{56,64},{64,7... | collective-permute-start | bytes 12296 | tf_op jit(solution)/shard_map/ppermute | solution.py:31
  98.5 7.0 %collective-permute-start.11 = (f32[2,4,128]{2,1,0:T(4,128)S(1)}, f32[2,4,128]{2,1,0:T(4,128)S(1)}, u32[]{:S(2)}, u32[]{:S(2)}) collective-permute-start(f32[2,4,128]{2,1,0:T(4,128)S(1)} %bitcast.157), channel_id=1, source_target_pairs={{0,120},{8,0},{16,8},{24,16},{32,24},{40,32},{48,40},{56,48},{64,5... | collective-permute-start | bytes 12296 | tf_op jit(solution)/shard_map/ppermute | solution.py:31
  115.8 17.9 %collective-permute-start.12 = (f32[128,1,256]{2,0,1:T(8,128)}, f32[128,1,256]{2,0,1:T(8,128)}, u32[]{:S(2)}, u32[]{:S(2)}) collective-permute-start(f32[128,1,256]{2,0,1:T(8,128)} %copy.185), channel_id=1, source_target_pairs={{8,0},{16,8},{24,16},{32,24},{40,32},{48,40},{56,48},{64,56},{72,6... | collective-permute-start | bytes 393224 | tf_op jit(solution)/shard_map/ppermute | solution.py:22
  121.9 18.8 %collective-permute-start.13 = (f32[128,1,256]{2,0,1:T(8,128)}, f32[128,1,256]{2,0,1:T(8,128)S(1)}, u32[]{:S(2)}, u32[]{:S(2)}) collective-permute-start(f32[128,1,256]{2,0,1:T(8,128)} %copy.187), channel_id=1, source_target_pairs={{0,8},{8,16},{16,24},{24,32},{32,40},{40,48},{48,56},{56,64},{64,7... | collective-permute-start | bytes 393224 | tf_op jit(solution)/shard_map/ppermute | solution.py:20
  121.9 24.7 %collective-permute-start.14 = (f32[128,16,1]{0,1,2:T(8,128)S(1)}, f32[128,16,1]{0,1,2:T(8,128)S(1)}, u32[]{:S(2)}, u32[]{:S(2)}) collective-permute-start(f32[128,16,1]{0,1,2:T(8,128)S(1)} %bitcast.156), channel_id=1, source_target_pairs={{1,0},{2,1},{3,2},{4,3},{5,4},{6,5},{7,6},{9,8},{10,9},{11,10},{12... | collective-permute-start | bytes 24584 | tf_op jit(solution)/shard_map/ppermute | solution.py:22
  123.8 22.9 %collective-permute-start.15 = (f32[128,16,1]{0,1,2:T(8,128)S(1)}, f32[128,16,1]{0,1,2:T(8,128)S(1)}, u32[]{:S(2)}, u32[]{:S(2)}) collective-permute-start(f32[128,16,1]{0,1,2:T(8,128)S(1)} %bitcast.155), channel_id=1, source_target_pairs={{0,1},{1,2},{2,3},{3,4},{4,5},{5,6},{6,7},{8,9},{9,10},{10,11},{11... | collective-permute-start | bytes 24584 | tf_op jit(solution)/shard_map/ppermute | solution.py:20
  131.7 20.2 %collective-permute-start.18 = (f32[64,8,1]{2,1,0:T(8,128)}, f32[64,8,1]{2,1,0:T(8,128)}, u32[]{:S(2)}, u32[]{:S(2)}) collective-permute-start(f32[64,8,1]{2,1,0:T(8,128)} %get-tuple-element.97), channel_id=1, source_target_pairs={{1,0},{2,1},{3,2},{4,3},{5,4},{6,5},{7,6},{9,8},{10,9},{11,10},{12... | collective-permute-start | bytes 6152 | tf_op jit(solution)/shard_map/ppermute | solution.py:22
  133.7 18.3 %collective-permute-start.19 = (f32[64,8,1]{2,1,0:T(8,128)}, f32[64,8,1]{2,1,0:T(8,128)}, u32[]{:S(2)}, u32[]{:S(2)}) collective-permute-start(f32[64,8,1]{2,1,0:T(8,128)} %get-tuple-element.98), channel_id=1, source_target_pairs={{0,1},{1,2},{2,3},{3,4},{4,5},{5,6},{6,7},{8,9},{9,10},{10,11},{11... | collective-permute-start | bytes 6152 | tf_op jit(solution)/shard_map/ppermute | solution.py:20
  141.4 10.6 %collective-permute-start.16 = (f32[64,1,512]{2,1,0:T(1,128)}, f32[64,1,512]{2,1,0:T(1,128)}, u32[]{:S(2)}, u32[]{:S(2)}) collective-permute-start(f32[64,1,512]{2,1,0:T(1,128)} %get-tuple-element.95), channel_id=1, source_target_pairs={{8,0},{16,8},{24,16},{32,24},{40,32},{48,40},{56,48},{64,56},{72,6... | collective-permute-start | bytes 393224 | tf_op jit(solution)/shard_map/ppermute | solution.py:22
  146.6 8.4 %collective-permute-start.17 = (f32[64,1,512]{2,1,0:T(1,128)}, f32[64,1,512]{2,1,0:T(1,128)}, u32[]{:S(2)}, u32[]{:S(2)}) collective-permute-start(f32[64,1,512]{2,1,0:T(1,128)} %get-tuple-element.96), channel_id=1, source_target_pairs={{0,8},{8,16},{16,24},{24,32},{32,40},{40,48},{48,56},{56,64},{64,7... | collective-permute-start | bytes 393224 | tf_op jit(solution)/shard_map/ppermute | solution.py:20
  (19 other events, 81.4 us)
where the time goes:
time: 159 us; the launch traced here: 158 us
  starting transfers between devices  61.7 us (39%)
  local copies, waits for them, and re-layouts  43.7 us (27%)
  other arithmetic  22.7 us (14%)
  matrix products  19.8 us (12%)
  waiting for transfers between devices  8.56 us (5%)
    ppermute x9, starting transfers between devices, extended(): lax.ppermute(head, axis, [((i + 1) % count, i) for i in range(ends)])  32 us
    ppermute x9, starting transfers between devices, extended(): lax.ppermute(tail, axis, [(i, (i + 1) % count) for i in range(ends)])  24 us
    unnamed x59, local copies, waits for them, and re-layouts  18.4 us
    slice x9, local copies, waits for them, and re-layouts, extended(): head = lax.slice_in_dim(cells, 0, width, axis=dim)  7.68 us
    dot_general x4, matrix products, columns(): jnp.dot(matrix, flat_field, precision=lax.Precision.HIGHEST, preferred_el...  7.45 us
    ppermute x9, waiting for transfers between devices, extended(): lax.ppermute(tail, axis, [(i, (i + 1) % count) for i in range(ends)])  7.22 us
    dot_general x2, matrix products, regrid_forward(): jnp.einsum('okij,fokj->foi', slot_tiles, picked, preferred_element_type=j...  6.22 us
    ppermute x2, starting transfers between devices, shifted(): lax.ppermute(shard, axis, [(i, (i + by) % devices) for i in range(devices)])  5.7 us
  transfers between devices with their start and end apart: 20, of which 4 were waited for; matrix products, arithmetic and copies ran while one was open for 24% of the time, Pallas kernels for 0%

commit v1 on v0

v1 whole, which is shorter than its diff:
```python
import functools

import jax
import jax.numpy as jnp
from jax import lax
from jax.experimental import pallas as pl
from jax.experimental.pallas import tpu as pltpu
from jax.sharding import PartitionSpec as P

FIELDS = 4
GAIN = 0.2
MESH = pl.DeviceIdType.MESH
f32, bf16 = jnp.float32, jnp.bfloat16


def split_cat(w):
    hi = w.astype(bf16)
    lo = (w - hi.astype(f32)).astype(bf16)
    return jnp.concatenate(
        [jnp.concatenate([hi, hi], axis=1), jnp.concatenate([lo, lo], axis=1)], axis=0
    )


def col(cat, field):
    n = field.shape[0]
    hi = field.astype(bf16)
    lo = (field - hi.astype(f32)).astype(bf16)
    r = jnp.dot(cat, jnp.concatenate([hi, lo], axis=0), preferred_element_type=f32)
    return r[:n] + r[n:]


def rounded(v):
    return v.astype(bf16).astype(f32)


def lane_shifts(v, lo, hi):
    n = v.shape[1]
    lane = lax.broadcasted_iota(jnp.int32, v.shape, 1)
    down = jnp.where(lane == 0, lo, pltpu.roll(v, 1, 1))
    up = jnp.where(lane == n - 1, hi, pltpu.roll(v, n - 1, 1))
    return down + up


def row_iota():
    return lax.broadcasted_iota(jnp.int32, (8, 128), 0)


def kernel(
    nx, ny, air_x, sea_x,
    av, sv, asc, ssc, aw, sw, wa, wo, mask, fidx, fcnt, ftil, sidx, scnt, stil,
    aout, sout,
    av_s, sv_s, as_s, ss_s, aw_s, sw_s, wa_s, wo_s, mask_s, fidx_s, fcnt_s, ft_s, sidx_s, scnt_s, st_s,
    wcat, wcat_t, ocat, ocat_t, mf,
    at, s1, adj, au, so, ao,
    dx_f, dx_s, S_a, S_o, L_f, L_s, F, G, A_f, A_s, Cf, Cs, R_f, R_s,
    xl_a, xr_a, xl_o, xr_o, e_lo, e_hi, h_lo, h_hi,
    xl2_a, xr2_a, xl2_o, xr2_o, e2_lo, e2_hi, h2_lo, h2_hi,
    in_sem, out_sem, send_sem, recv_sem,
):
    gx, gy = lax.axis_index("gx"), lax.axis_index("gy")
    right, left = lax.rem(gx + 1, nx), lax.rem(gx + nx - 1, nx)
    above, below = lax.rem(gy + 1, ny), lax.rem(gy + ny - 1, ny)
    to_right, to_left = (right, gy), (left, gy)
    to_above, to_below = (gx, above), (gx, below)

    def load_columns(src, dst, sem, count):
        for x in range(count):
            pltpu.make_async_copy(src.at[:, x, :], dst.at[x], in_sem.at[sem]).start()

    def loaded(dst, sem):
        pltpu.make_async_copy(dst, dst, in_sem.at[sem]).wait()

    def load(src, dst, sem):
        pltpu.make_async_copy(src, dst, in_sem.at[sem]).start()

    barrier = pltpu.get_barrier_semaphore()
    for device in (to_right, to_left, to_above, to_below):
        pl.semaphore_signal(barrier, inc=1, device_id=device, device_id_type=MESH)

    load(mask, mask_s, 0)
    load_columns(sv, sv_s, 1, sea_x)
    load_columns(av, av_s, 2, air_x)
    load(wa, wa_s, 3)
    load(wo, wo_s, 4)
    load(fidx.at[0], fidx_s, 5)
    load(fcnt, fcnt_s, 6)
    load(sidx.at[0], sidx_s, 7)
    load(scnt, scnt_s, 8)
    load_columns(asc, as_s, 9, air_x)
    load(ftil.at[0], ft_s, 10)
    load(stil.at[0], st_s, 11)
    load_columns(ssc, ss_s, 12, sea_x)
    load_columns(sw, sw_s, 13, sea_x)
    load_columns(aw, aw_s, 14, air_x)

    pl.semaphore_wait(barrier, 4)

    def remote(src, dst, k, device):
        return pltpu.make_async_remote_copy(
            src_ref=src, dst_ref=dst, send_sem=send_sem.at[k], recv_sem=recv_sem.at[k],
            device_id=device, device_id_type=MESH,
        )

    halo_xr = remote(av.at[:, air_x - 1, :], xl_a, 0, to_right)
    halo_xl = remote(av.at[:, 0, :], xr_a, 1, to_left)
    halo_xr.start()
    halo_xl.start()

    loaded(mask_s, 0)
    mf[...] = mask_s[...].astype(f32)
    loaded(sv_s, 1)

    lane64 = lax.broadcasted_iota(jnp.int32, (64, 128), 1)
    zero64 = jnp.zeros((64, 128), f32)

    def sea_zero(x, acc):
        lo, hi = acc
        z = mf[pl.ds(x, 1), :] * sv_s[x]
        sv_s[x] = z
        here = lane64 == x + 2 * air_x
        lo = jnp.where(here, z[:, 0:1], lo)
        hi = jnp.where(here, z[:, -1:], hi)
        return lo, hi

    edges = lax.fori_loop(0, sea_x, sea_zero, (zero64, zero64))
    halo_or = remote(sv_s.at[sea_x - 1], xl_o, 2, to_right)
    halo_ol = remote(sv_s.at[0], xr_o, 3, to_left)
    halo_or.start()
    halo_ol.start()

    loaded(av_s, 2)

    def pack_air(field, x, acc):
        lo, hi = acc
        for part in range(2):
            v = field[64 * part:64 * part + 64]
            here = lane64 == x + part * air_x
            lo = jnp.where(here, v[:, 0:1], lo)
            hi = jnp.where(here, v[:, -1:], hi)
        return lo, hi

    edges = lax.fori_loop(0, air_x, lambda x, acc: pack_air(av_s[x], x, acc), edges)
    e_lo[...], e_hi[...] = edges
    halo_yu = remote(e_hi, h_lo, 4, to_above)
    halo_yd = remote(e_lo, h_hi, 5, to_below)
    halo_yu.start()
    halo_yd.start()

    loaded(wa_s, 3)
    loaded(wo_s, 4)
    wcat[...] = split_cat(wa_s[...])
    wcat_t[...] = split_cat(wa_s[...].T)
    ocat[...] = split_cat(wo_s[...])
    ocat_t[...] = split_cat(wo_s[...].T)

    row_blocks = 32 * nx

    def places(idx_s, cnt_s, dx):
        own = gx * 32 + lax.broadcasted_iota(jnp.int32, (4, 32), 1)
        rel = idx_s[...] - own
        d = jnp.where(rel == 0, 0.0, jnp.where((rel == 1) | (rel == 1 - row_blocks), 1.0, -1.0))
        block = lax.broadcasted_iota(jnp.int32, (128, 32), 0) // 4
        pick = jnp.where(block == lax.broadcasted_iota(jnp.int32, (128, 32), 1), 1.0, 0.0)
        count = cnt_s[...].astype(f32)
        for k in range(4):
            dk = jnp.where(count > k, d[k:k + 1, :], 2.0)
            dx[k] = jnp.broadcast_to(jnp.sum(pick * dk, axis=1, keepdims=True), (128, 128))

    loaded(fidx_s, 5)
    loaded(fcnt_s, 6)
    places(fidx_s, fcnt_s, dx_f)
    loaded(sidx_s, 7)
    loaded(scnt_s, 8)
    places(sidx_s, scnt_s, dx_s)

    halo_xl.wait()
    halo_xr.wait()
    halo_ol.wait()
    halo_or.wait()
    halo_yu.wait()
    halo_yd.wait()

    def zero_outside(h):
        lo = jnp.where(gy == 0, 0.0, h[0][...])
        hi = jnp.where(gy == ny - 1, 0.0, h[1][...])
        h[0][...] = lo
        h[1][...] = hi

    zero_outside((h_lo, h_hi))

    def pick_lane(packed, lane):
        return jnp.sum(jnp.where(lane64 == lane, packed, 0.0), axis=1, keepdims=True)

    def air_ends(hl, hh, x):
        lo = jnp.concatenate([pick_lane(hl[...], x), pick_lane(hl[...], x + air_x)], axis=0)
        hi = jnp.concatenate([pick_lane(hh[...], x), pick_lane(hh[...], x + air_x)], axis=0)
        return lo, hi

    def sea_ends(hl, hh, x):
        return pick_lane(hl[...], x + 2 * air_x), pick_lane(hh[...], x + 2 * air_x)

    loaded(as_s, 9)
    half = row_iota() < 4

    def air_first(x, west, east):
        v = av_s[x]
        lo, hi = air_ends(h_lo, h_hi, x)
        one = GAIN * (v + west + east + lane_shifts(v, lo, hi))
        two = col(wcat[...], as_s[x] * one)
        at[x] = two
        low = rounded(two[120:128])
        slab = jnp.where(half, pltpu.roll(low[:, 0:128], 4, 0), low[:, 128:256])
        S_a[pl.ds(pl.multiple_of(8 + 8 * x, 8), 8), :] = slab

    air_first(0, xl_a[...], av_s[1])
    air_first(air_x - 1, av_s[air_x - 2], xr_a[...])

    def send_rims(src_hi, src_lo, dst_hi, dst_lo, k):
        up = remote(src_hi.at[128:136], dst_hi.at[0:8], k, to_right)
        down = remote(src_lo.at[8:16], dst_lo.at[136:144], k + 1, to_left)
        up.start()
        down.start()
        return up, down

    rim_a = send_rims(S_a, S_a, S_a, S_a, 6)

    def sea_first(x, west, east):
        v = sv_s[x]
        m = mf[pl.ds(x, 1), :]
        lo, hi = sea_ends(h_lo, h_hi, x)
        one = v + (GAIN * m) * (west + east + lane_shifts(v, lo, hi) - 4.0 * v)
        s1[x] = one
        top = rounded(one[0:8])
        for q in range(2):
            a = top[:, 256 * q:256 * q + 128]
            b = top[:, 256 * q + 128:256 * q + 256]
            slab = jnp.where(half, a, pltpu.roll(b, 4, 0))
            S_o[pl.ds(pl.multiple_of(8 + 16 * x + 8 * q, 8), 8), :] = slab

    sea_first(0, xl_o[...], sv_s[1])
    sea_first(sea_x - 1, sv_s[sea_x - 2], xr_o[...])
    rim_o = send_rims(S_o, S_o, S_o, S_o, 8)

    @pl.loop(1, sea_x - 1)
    def _(x):
        sea_first(x, sv_s[x - 1], sv_s[x + 1])

    @pl.loop(1, air_x - 1)
    def _(x):
        air_first(x, av_s[x - 1], av_s[x + 1])

    def gather_rows(S, dx, L, r0, r1):
        s_m, s_0, s_p = S[4 + r0:4 + r1], S[8 + r0:8 + r1], S[12 + r0:12 + r1]
        for k in range(4):
            d = dx[k, r0:r1]
            L[r0:r1, 128 * k:128 * k + 128] = jnp.where(
                d == 0.0, s_0, jnp.where(d == -1.0, s_m, jnp.where(d == 1.0, s_p, 0.0))
            )

    def pair_tiles(T, p):
        return jnp.concatenate(
            [jnp.concatenate([T[2 * p + a, k] for k in range(4)], axis=1) for a in range(2)], axis=0
        )

    def pair_rows(p):
        return pl.ds(pl.multiple_of(8 * p, 8), 8)

    def forward_pair(L, T, out, p):
        r = lax.dot_general(
            L[pair_rows(p), :].astype(bf16), pair_tiles(T, p), (((1,), (1,)), ((), ())),
            preferred_element_type=f32,
        )
        out[pair_rows(p), :] = jnp.where(half, r[:, 0:128], r[:, 128:256])

    def back_pair(A, T, dx, C, p):
        a = A[pair_rows(p), :]
        lhs = jnp.concatenate([jnp.where(half, a, 0.0), jnp.where(half, 0.0, a)], axis=1)
        r = jnp.dot(lhs.astype(bf16), pair_tiles(T, p), preferred_element_type=f32)
        sums = [jnp.zeros((8, 128), f32) for _ in range(3)]
        for k in range(4):
            d = dx[k, pair_rows(p), :]
            c = r[:, 128 * k:128 * k + 128]
            for n in range(3):
                sums[n] = sums[n] + jnp.where(d == n - 1.0, c, 0.0)
        for n in range(3):
            C[n, pl.ds(pl.multiple_of(8 + 8 * p, 8), 8), :] = sums[n]

    gather_rows(S_a, dx_f, L_f, 8, 120)
    gather_rows(S_o, dx_s, L_s, 8, 120)
    loaded(ft_s, 10)
    loaded(st_s, 11)

    @pl.loop(1, 15)
    def _(p):
        forward_pair(L_f, ft_s, F, p)
        forward_pair(L_s, st_s, G, p)

    for c in rim_a + rim_o:
        c.wait()
    for r0 in (0, 120):
        gather_rows(S_a, dx_f, L_f, r0, r0 + 8)
        gather_rows(S_o, dx_s, L_s, r0, r0 + 8)
    for p in (0, 15):
        forward_pair(L_f, ft_s, F, p)
        forward_pair(L_s, st_s, G, p)

    loaded(ss_s, 12)
    loaded(sw_s, 13)

    def sea_top(slabs):
        parts = []
        for slab in slabs:
            parts.append(jnp.where(half, slab, 0.0))
            parts.append(jnp.where(half, pltpu.roll(slab, 4, 0), 0.0))
        return jnp.concatenate(parts, axis=1)

    def sea_slabs(ref, x):
        return [ref[pl.ds(pl.multiple_of(16 * x + 8 * q, 8), 8), :] for q in range(2)]

    def sea_columns(x):
        m = mf[pl.ds(x, 1), :]
        one = s1[x]
        two = jnp.concatenate([one[0:8] + m * sea_top(sea_slabs(F, x)), one[8:]], axis=0)
        three = col(ocat[...], ss_s[x] * two)
        back = ss_s[x] * col(ocat_t[...], m * (sw_s[x] * three))
        adj[x] = back
        top = rounded(m * back[0:8])
        for q in range(2):
            a = top[:, 256 * q:256 * q + 128]
            b = top[:, 256 * q + 128:256 * q + 256]
            A_f[pl.ds(pl.multiple_of(16 * x + 8 * q, 8), 8), :] = jnp.where(half, a, pltpu.roll(b, 4, 0))

    sea_columns(0)
    sea_columns(sea_x - 1)
    for p in (0, 15):
        back_pair(A_f, ft_s, dx_f, Cf, p)
    rim_f = send_rims(Cf.at[2], Cf.at[0], Cf.at[2], Cf.at[0], 10)

    loaded(aw_s, 14)

    def air_low(ref, x):
        slab = ref[pl.ds(pl.multiple_of(8 * x, 8), 8), :]
        return jnp.concatenate(
            [jnp.where(half, 0.0, pltpu.roll(slab, 4, 0)), jnp.where(half, 0.0, slab)], axis=1
        )

    def air_forcing(x):
        two = at[x]
        three = jnp.concatenate([two[0:120], two[120:128] + air_low(G, x)], axis=0)
        forcing = aw_s[x] * three
        at[x] = forcing
        low = rounded(forcing[120:128])
        A_s[pl.ds(pl.multiple_of(8 * x, 8), 8), :] = jnp.where(
            half, pltpu.roll(low[:, 0:128], 4, 0), low[:, 128:256]
        )

    air_forcing(0)
    air_forcing(air_x - 1)
    for p in (0, 15):
        back_pair(A_s, st_s, dx_s, Cs, p)
    rim_s = send_rims(Cs.at[2], Cs.at[0], Cs.at[2], Cs.at[0], 12)

    @pl.loop(1, sea_x - 1)
    def _(x):
        sea_columns(x)

    @pl.loop(1, air_x - 1)
    def _(x):
        air_forcing(x)

    @pl.loop(1, 15)
    def _(p):
        back_pair(A_f, ft_s, dx_f, Cf, p)
        back_pair(A_s, st_s, dx_s, Cs, p)

    for c in rim_f + rim_s:
        c.wait()
    R_f[...] = Cf[1, 8:136] + Cf[0, 12:140] + Cf[2, 4:132]
    R_s[...] = Cs[1, 8:136] + Cs[0, 12:140] + Cs[2, 4:132]

    def sea_upper(x):
        back = adj[x]
        up = jnp.concatenate([back[0:8] + sea_top(sea_slabs(R_s, x)), back[8:]], axis=0)
        z = mf[pl.ds(x, 1), :] * up
        adj[x] = z
        return z

    def air_upper(x):
        low = at[x]
        low = jnp.concatenate([low[0:120], low[120:128] + air_low(R_f, x)], axis=0)
        up = as_s[x] * col(wcat_t[...], low)
        au[x] = up
        return up

    def pack_sea(z, x, acc):
        lo, hi = acc
        here = lane64 == x + 2 * air_x
        return jnp.where(here, z[:, 0:1], lo), jnp.where(here, z[:, -1:], hi)

    edges = (zero64, zero64)
    for x in (0, sea_x - 1):
        edges = pack_sea(sea_upper(x), x, edges)
    for x in (0, air_x - 1):
        edges = pack_air(air_upper(x), x, edges)
    last = [
        remote(au.at[air_x - 1], xl2_a, 14, to_right),
        remote(au.at[0], xr2_a, 15, to_left),
        remote(adj.at[sea_x - 1], xl2_o, 16, to_right),
        remote(adj.at[0], xr2_o, 17, to_left),
    ]
    for c in last:
        c.start()
    edges = lax.fori_loop(1, sea_x - 1, lambda x, acc: pack_sea(sea_upper(x), x, acc), edges)
    edges = lax.fori_loop(1, air_x - 1, lambda x, acc: pack_air(air_upper(x), x, acc), edges)
    e2_lo[...], e2_hi[...] = edges
    last += [remote(e2_hi, h2_lo, 18, to_above), remote(e2_lo, h2_hi, 19, to_below)]
    for c in last[4:]:
        c.start()
    for c in last:
        c.wait()
    zero_outside((h2_lo, h2_hi))

    def sea_last(x, west, east):
        z = adj[x]
        lo, hi = sea_ends(h2_lo, h2_hi, x)
        so[x] = z + (GAIN * mf[pl.ds(x, 1), :]) * (west + east + lane_shifts(z, lo, hi) - 4.0 * z)

    def air_last(x, west, east):
        v = au[x]
        lo, hi = air_ends(h2_lo, h2_hi, x)
        ao[x] = GAIN * (v + west + east + lane_shifts(v, lo, hi))

    sea_last(0, xl2_o[...], adj[1])
    sea_last(sea_x - 1, adj[sea_x - 2], xr2_o[...])

    @pl.loop(1, sea_x - 1)
    def _(x):
        sea_last(x, adj[x - 1], adj[x + 1])

    for x in range(sea_x):
        pltpu.make_async_copy(so.at[x], sout.at[:, x, :], out_sem.at[0]).start()

    air_last(0, xl2_a[...], au[1])
    air_last(air_x - 1, au[air_x - 2], xr2_a[...])

    @pl.loop(1, air_x - 1)
    def _(x):
        air_last(x, au[x - 1], au[x + 1])

    for x in range(air_x):
        pltpu.make_async_copy(ao.at[x], aout.at[:, x, :], out_sem.at[1]).start()
    pltpu.make_async_copy(so, so, out_sem.at[0]).wait()
    pltpu.make_async_copy(ao, ao, out_sem.at[1]).wait()


def shards(*args, nx, ny):
    av, sv = args[0], args[1]
    args = [a.transpose(0, 2, 1) if n in (9, 12) else a for n, a in enumerate(args)]
    levels, air_x, air_y = av.shape
    sea_levels, sea_x, sea_y = sv.shape
    V = pltpu.VMEM
    air = V((air_x, levels, air_y), f32)
    sea = V((sea_x, sea_levels, sea_y), f32)
    blk = V((128, 128), f32)
    ext = V((144, 128), f32)
    rowa, rowo, pack = V((levels, air_y), f32), V((sea_levels, sea_y), f32), V((64, 128), f32)
    tiles = V((32, 4, 128, 128), bf16)
    idx, cnt = V((4, 32), jnp.int32), V((1, 32), jnp.int32)
    wcat = V((2 * levels, 2 * levels), bf16)
    ocat = V((2 * sea_levels, 2 * sea_levels), bf16)
    dx = V((4, 128, 128), f32)
    cterm = V((3, 144, 128), f32)
    dma = pltpu.SemaphoreType.DMA
    scratch = [
        air, sea, air, sea, air, sea, V((levels, levels), f32), V((sea_levels, sea_levels), f32),
        V((sea_x, sea_y), jnp.int32), idx, cnt, tiles, idx, cnt, tiles,
        wcat, wcat, ocat, ocat, V((sea_x, sea_y), f32),
        air, sea, sea, air, sea, air,
        dx, dx, ext, ext, V((128, 512), f32), V((128, 512), f32), blk, blk, blk, blk, cterm, cterm, blk, blk,
        rowa, rowa, rowo, rowo, pack, pack, pack, pack,
        rowa, rowa, rowo, rowo, pack, pack, pack, pack,
        dma((15,)), dma((2,)), dma((20,)), dma((20,)),
    ]
    anywhere = pl.BlockSpec(memory_space=pl.ANY)
    return pl.pallas_call(
        functools.partial(kernel, nx, ny, air_x, sea_x),
        out_shape=(jax.ShapeDtypeStruct(av.shape, f32), jax.ShapeDtypeStruct(sv.shape, f32)),
        in_specs=[anywhere] * 15,
        out_specs=(anywhere, anywhere),
        scratch_shapes=scratch,
        compiler_params=pltpu.CompilerParams(
            collective_id=0, has_side_effects=True, vmem_limit_bytes=56 * 1024 * 1024
        ),
        cost_estimate=pl.CostEstimate(flops=4_000_000_000, bytes_accessed=21_000_000, transcendentals=0),
    )(*args)


def solution(mesh):
    grid = P(None, "gx", "gy")
    index, count, tiles = P("gy", "gx", None), P("gy", "gx"), P("gy", "gx", None, None, None)
    return jax.shard_map(
        functools.partial(shards, nx=mesh.shape["gx"], ny=mesh.shape["gy"]),
        mesh=mesh,
        in_specs=(grid,) * 6 + (P(), P(), P("gx", "gy"), index, count, tiles, index, count, tiles),
        out_specs=(grid, grid),
        check_vma=False,
    )
```

time: 159 us -> 52.6 us (0.33)
  the two profiles are of different devices: /device:TPU:96 before, /device:TPU:0 now
where the time goes in v1:
time: 52.6 us; the launch traced here: 52.1 us
  Pallas kernels  47.3 us (90%)
  local copies, waits for them, and re-layouts  4.14 us (8%)
  between operations  0.65 us (1%)
    pallas_call x1, Pallas kernels, shards(): pl.pallas_call(functools.partial(kernel, nx, ny, air_x, sea_x), out_shape...  47.3 us
    unnamed x4, local copies, waits for them, and re-layouts  4.14 us

profile of v1, /device:TPU:0, one launch (start us, length us, event | category | flops | bytes accessed | tf_op | source)
XLA Modules:
  0.0 52.1 jit_solution(17332023846737280905)
XLA Ops:
  0.6 47.3 %shard_map.158 = (f32[128,16,256]{2,1,0:T(8,128)}, f32[64,8,512]{2,1,0:T(8,128)}) custom-call(f32[128,16,256]{2,1,0:T(8,128)} %av.1, f32[64,8,512]{2,1,0:T(8,128)} %sv.1, f32[128,16,256]{2,1,0:T(8,128)} %asc.1, f32[64,8,512]{2,1,0:T(8,128)} %ssc.1, f32[128,16,256]{2,1,0:T(8,128)} %aw.1, f32[64,8,512]{2,1,0:T(8,128)} %sw.1, f32[128,128]{1,0:T(8,128)} %wa.1, ...), custom_call_target="tpu_custom_call" | custom-call | flops 4000000000 | bytes 21000000 | tf_op jit(solution)/shard_map/pallas_call | solution.py:485
  48.0 0.0 copy-start
  48.0 3.2 %copy.19 = f32[128,16,256]{2,1,0:T(8,128)} copy(f32[128,16,256]{2,1,0:T(8,128)} %get-tuple-element.4) | data formatting | bytes 4194304
  51.2 0.0 copy-done
  51.2 1.0 %copy.20 = f32[64,8,512]{2,1,0:T(8,128)} copy(f32[64,8,512]{2,1,0:T(8,128)S(1)} %copy-done) | data formatting | bytes 2097152
Async XLA Ops:
  48.0 3.2 %copy-start = (f32[64,8,512]{2,1,0:T(8,128)S(1)}, f32[64,8,512]{2,1,0:T(8,128)}, u32[]{:S(2)}) copy-start(f32[64,8,512]{2,1,0:T(8,128)} %get-tuple-element.5) | copy-start | bytes 3145732

commit v2 on v1

--- a/solution.py
+++ b/solution.py
@@ -115,14 +115,16 @@
 
     def sea_zero(x, acc):
         lo, hi = acc
-        z = mf[pl.ds(x, 1), :] * sv_s[x]
+        z = mf[x:x + 1, :] * sv_s[x]
         sv_s[x] = z
         here = lane64 == x + 2 * air_x
         lo = jnp.where(here, z[:, 0:1], lo)
         hi = jnp.where(here, z[:, -1:], hi)
         return lo, hi
 
-    edges = lax.fori_loop(0, sea_x, sea_zero, (zero64, zero64))
+    edges = (zero64, zero64)
+    for x in range(sea_x):
+        edges = sea_zero(x, edges)
     halo_or = remote(sv_s.at[sea_x - 1], xl_o, 2, to_right)
     halo_ol = remote(sv_s.at[0], xr_o, 3, to_left)
     halo_or.start()
@@ -139,7 +141,8 @@
             hi = jnp.where(here, v[:, -1:], hi)
         return lo, hi
 
-    edges = lax.fori_loop(0, air_x, lambda x, acc: pack_air(av_s[x], x, acc), edges)
+    for x in range(air_x):
+        edges = pack_air(av_s[x], x, edges)
     e_lo[...], e_hi[...] = edges
     halo_yu = remote(e_hi, h_lo, 4, to_above)
     halo_yd = remote(e_lo, h_hi, 5, to_below)
@@ -189,7 +192,7 @@
     zero_outside((h_lo, h_hi))
 
     def pick_lane(packed, lane):
-        return jnp.sum(jnp.where(lane64 == lane, packed, 0.0), axis=1, keepdims=True)
+        return packed[:, lane:lane + 1]
 
     def air_ends(hl, hh, x):
         lo = jnp.concatenate([pick_lane(hl[...], x), pick_lane(hl[...], x + air_x)], axis=0)
@@ -210,7 +213,7 @@
         at[x] = two
         low = rounded(two[120:128])
         slab = jnp.where(half, pltpu.roll(low[:, 0:128], 4, 0), low[:, 128:256])
-        S_a[pl.ds(pl.multiple_of(8 + 8 * x, 8), 8), :] = slab
+        S_a[pl.ds(8 + 8 * x, 8), :] = slab
 
     air_first(0, xl_a[...], av_s[1])
     air_first(air_x - 1, av_s[air_x - 2], xr_a[...])
@@ -226,7 +229,7 @@
 
     def sea_first(x, west, east):
         v = sv_s[x]
-        m = mf[pl.ds(x, 1), :]
+        m = mf[x:x + 1, :]
         lo, hi = sea_ends(h_lo, h_hi, x)
         one = v + (GAIN * m) * (west + east + lane_shifts(v, lo, hi) - 4.0 * v)
         s1[x] = one
@@ -235,18 +238,16 @@
             a = top[:, 256 * q:256 * q + 128]
             b = top[:, 256 * q + 128:256 * q + 256]
             slab = jnp.where(half, a, pltpu.roll(b, 4, 0))
-            S_o[pl.ds(pl.multiple_of(8 + 16 * x + 8 * q, 8), 8), :] = slab
+            S_o[pl.ds(8 + 16 * x + 8 * q, 8), :] = slab
 
     sea_first(0, xl_o[...], sv_s[1])
     sea_first(sea_x - 1, sv_s[sea_x - 2], xr_o[...])
     rim_o = send_rims(S_o, S_o, S_o, S_o, 8)
 
-    @pl.loop(1, sea_x - 1)
-    def _(x):
+    for x in range(1, sea_x - 1):
         sea_first(x, sv_s[x - 1], sv_s[x + 1])
 
-    @pl.loop(1, air_x - 1)
-    def _(x):
+    for x in range(1, air_x - 1):
         air_first(x, av_s[x - 1], av_s[x + 1])
 
     def gather_rows(S, dx, L, r0, r1):
@@ -263,7 +264,7 @@
         )
 
     def pair_rows(p):
-        return pl.ds(pl.multiple_of(8 * p, 8), 8)
+        return pl.ds(8 * p, 8)
 
     def forward_pair(L, T, out, p):
         r = lax.dot_general(
@@ -283,15 +284,14 @@
             for n in range(3):
                 sums[n] = sums[n] + jnp.where(d == n - 1.0, c, 0.0)
         for n in range(3):
-            C[n, pl.ds(pl.multiple_of(8 + 8 * p, 8), 8), :] = sums[n]
+            C[n, pl.ds(8 + 8 * p, 8), :] = sums[n]
 
     gather_rows(S_a, dx_f, L_f, 8, 120)
     gather_rows(S_o, dx_s, L_s, 8, 120)
     loaded(ft_s, 10)
     loaded(st_s, 11)
 
-    @pl.loop(1, 15)
-    def _(p):
+    for p in range(1, 15):
         forward_pair(L_f, ft_s, F, p)
         forward_pair(L_s, st_s, G, p)
 
@@ -315,10 +315,10 @@
         return jnp.concatenate(parts, axis=1)
 
     def sea_slabs(ref, x):
-        return [ref[pl.ds(pl.multiple_of(16 * x + 8 * q, 8), 8), :] for q in range(2)]
+        return [ref[pl.ds(16 * x + 8 * q, 8), :] for q in range(2)]
 
     def sea_columns(x):
-        m = mf[pl.ds(x, 1), :]
+        m = mf[x:x + 1, :]
         one = s1[x]
         two = jnp.concatenate([one[0:8] + m * sea_top(sea_slabs(F, x)), one[8:]], axis=0)
         three = col(ocat[...], ss_s[x] * two)
@@ -328,7 +328,7 @@
         for q in range(2):
             a = top[:, 256 * q:256 * q + 128]
             b = top[:, 256 * q + 128:256 * q + 256]
-            A_f[pl.ds(pl.multiple_of(16 * x + 8 * q, 8), 8), :] = jnp.where(half, a, pltpu.roll(b, 4, 0))
+            A_f[pl.ds(16 * x + 8 * q, 8), :] = jnp.where(half, a, pltpu.roll(b, 4, 0))
 
     sea_columns(0)
     sea_columns(sea_x - 1)
@@ -339,7 +339,7 @@
     loaded(aw_s, 14)
 
     def air_low(ref, x):
-        slab = ref[pl.ds(pl.multiple_of(8 * x, 8), 8), :]
+        slab = ref[pl.ds(8 * x, 8), :]
         return jnp.concatenate(
             [jnp.where(half, 0.0, pltpu.roll(slab, 4, 0)), jnp.where(half, 0.0, slab)], axis=1
         )
@@ -350,7 +350,7 @@
         forcing = aw_s[x] * three
         at[x] = forcing
         low = rounded(forcing[120:128])
-        A_s[pl.ds(pl.multiple_of(8 * x, 8), 8), :] = jnp.where(
+        A_s[pl.ds(8 * x, 8), :] = jnp.where(
             half, pltpu.roll(low[:, 0:128], 4, 0), low[:, 128:256]
         )
 
@@ -360,16 +360,13 @@
         back_pair(A_s, st_s, dx_s, Cs, p)
     rim_s = send_rims(Cs.at[2], Cs.at[0], Cs.at[2], Cs.at[0], 12)
 
-    @pl.loop(1, sea_x - 1)
-    def _(x):
+    for x in range(1, sea_x - 1):
         sea_columns(x)
 
-    @pl.loop(1, air_x - 1)
-    def _(x):
+    for x in range(1, air_x - 1):
         air_forcing(x)
 
-    @pl.loop(1, 15)
-    def _(p):
+    for p in range(1, 15):
         back_pair(A_f, ft_s, dx_f, Cf, p)
         back_pair(A_s, st_s, dx_s, Cs, p)
 
@@ -381,7 +378,7 @@
     def sea_upper(x):
         back = adj[x]
         up = jnp.concatenate([back[0:8] + sea_top(sea_slabs(R_s, x)), back[8:]], axis=0)
-        z = mf[pl.ds(x, 1), :] * up
+        z = mf[x:x + 1, :] * up
         adj[x] = z
         return z
 
@@ -410,8 +407,10 @@
     ]
     for c in last:
         c.start()
-    edges = lax.fori_loop(1, sea_x - 1, lambda x, acc: pack_sea(sea_upper(x), x, acc), edges)
-    edges = lax.fori_loop(1, air_x - 1, lambda x, acc: pack_air(air_upper(x), x, acc), edges)
+    for x in range(1, sea_x - 1):
+        edges = pack_sea(sea_upper(x), x, edges)
+    for x in range(1, air_x - 1):
+        edges = pack_air(air_upper(x), x, edges)
     e2_lo[...], e2_hi[...] = edges
     last += [remote(e2_hi, h2_lo, 18, to_above), remote(e2_lo, h2_hi, 19, to_below)]
     for c in last[4:]:
@@ -423,7 +422,7 @@
     def sea_last(x, west, east):
         z = adj[x]
         lo, hi = sea_ends(h2_lo, h2_hi, x)
-        so[x] = z + (GAIN * mf[pl.ds(x, 1), :]) * (west + east + lane_shifts(z, lo, hi) - 4.0 * z)
+        so[x] = z + (GAIN * mf[x:x + 1, :]) * (west + east + lane_shifts(z, lo, hi) - 4.0 * z)
 
     def air_last(x, west, east):
         v = au[x]
@@ -433,8 +432,7 @@
     sea_last(0, xl2_o[...], adj[1])
     sea_last(sea_x - 1, adj[sea_x - 2], xr2_o[...])
 
-    @pl.loop(1, sea_x - 1)
-    def _(x):
+    for x in range(1, sea_x - 1):
         sea_last(x, adj[x - 1], adj[x + 1])
 
     for x in range(sea_x):
@@ -443,8 +441,7 @@
     air_last(0, xl2_a[...], au[1])
     air_last(air_x - 1, au[air_x - 2], xr2_a[...])
 
-    @pl.loop(1, air_x - 1)
-    def _(x):
+    for x in range(1, air_x - 1):
         air_last(x, au[x - 1], au[x + 1])
 
     for x in range(air_x):

time: 52.6 us -> 42 us (0.80)
  Pallas kernels: 47.3 us -> 37.1 us
    pallas_call x1, Pallas kernels: 47.3 us -> 37.1 us  [shards(): pl.pallas_call(functools.partial(kernel, nx, ny, air_x, sea_x), out_shape...]
where the time goes in v2:
time: 42 us; the launch traced here: 41.9 us
  Pallas kernels  37.1 us (88%)
  local copies, waits for them, and re-layouts  4.14 us (10%)
  between operations  0.65 us (2%)
    pallas_call x1, Pallas kernels, shards(): pl.pallas_call(functools.partial(kernel, nx, ny, air_x, sea_x), out_shape...  37.1 us
    unnamed x4, local copies, waits for them, and re-layouts  4.14 us

profile of v2, /device:TPU:0, one launch (start us, length us, event | category | flops | bytes accessed | tf_op | source)
XLA Modules:
  0.0 41.9 jit_solution(14894711685039403625)
XLA Ops:
  0.6 37.1 %shard_map.158 = (f32[128,16,256]{2,1,0:T(8,128)}, f32[64,8,512]{2,1,0:T(8,128)}) custom-call(f32[128,16,256]{2,1,0:T(8,128)} %av.1, f32[64,8,512]{2,1,0:T(8,128)} %sv.1, f32[128,16,256]{2,1,0:T(8,128)} %asc.1, f32[64,8,512]{2,1,0:T(8,128)} %ssc.1, f32[128,16,256]{2,1,0:T(8,128)} %aw.1, f32[64,8,512]{2,1,0:T(8,128)} %sw.1, f32[128,128]{1,0:T(8,128)} %wa.1, ...), custom_call_target="tpu_custom_call" | custom-call | flops 4000000000 | bytes 21000000 | tf_op jit(solution)/shard_map/pallas_call | solution.py:482
  37.7 0.0 copy-start
  37.7 3.2 %copy.19 = f32[128,16,256]{2,1,0:T(8,128)} copy(f32[128,16,256]{2,1,0:T(8,128)} %get-tuple-element.4) | data formatting | bytes 4194304
  40.9 0.0 copy-done
  40.9 1.0 %copy.20 = f32[64,8,512]{2,1,0:T(8,128)} copy(f32[64,8,512]{2,1,0:T(8,128)S(1)} %copy-done) | data formatting | bytes 2097152
Async XLA Ops:
  37.7 3.2 %copy-start = (f32[64,8,512]{2,1,0:T(8,128)S(1)}, f32[64,8,512]{2,1,0:T(8,128)}, u32[]{:S(2)}) copy-start(f32[64,8,512]{2,1,0:T(8,128)} %get-tuple-element.5) | copy-start | bytes 3145732

commit v3 on v2

v3 whole, which is shorter than its diff:
```python
import functools

import jax
import jax.numpy as jnp
from jax import lax
from jax.experimental import pallas as pl
from jax.experimental.pallas import tpu as pltpu
from jax.sharding import PartitionSpec as P

GAIN = 0.2
MESH = pl.DeviceIdType.MESH
f32, bf16 = jnp.float32, jnp.bfloat16


def split_cat(w):
    hi = w.astype(bf16)
    lo = (w - hi.astype(f32)).astype(bf16)
    return jnp.concatenate(
        [jnp.concatenate([hi, hi], axis=1), jnp.concatenate([lo, lo], axis=1)], axis=0
    )


def col(cat, field):
    n = field.shape[0]
    hi = field.astype(bf16)
    lo = (field - hi.astype(f32)).astype(bf16)
    r = jnp.dot(cat, jnp.concatenate([hi, lo], axis=0), preferred_element_type=f32)
    return r[:n] + r[n:]


def rounded(v):
    return v.astype(bf16).astype(f32)


def lane_of(v):
    return lax.broadcasted_iota(jnp.int32, v.shape, 1)


def lane_shifts(v):
    n = v.shape[1]
    lane = lane_of(v)
    down = jnp.where(lane == 0, 0.0, pltpu.roll(v, 1, 1))
    up = jnp.where(lane == n - 1, 0.0, pltpu.roll(v, n - 1, 1))
    return down + up


def with_ends(v, lo, hi):
    head, tail = v[:, :128], v[:, -128:]
    lane = lane_of(head)
    head = jnp.where(lane == 0, head + lo, head)
    tail = jnp.where(lane == 127, tail + hi, tail)
    return jnp.concatenate([head, v[:, 128:-128], tail], axis=1) if v.shape[1] > 256 else jnp.concatenate(
        [head, tail], axis=1
    )


def put_ends(packed, field, lo, hi):
    lane = lane_of(packed)
    packed = jnp.where(lane == lo, field[:, 0:1], packed)
    return jnp.where(lane == hi, field[:, -1:], packed)


def kernel(
    nx, ny, air_x, sea_x,
    av, sv, asc, ssc, aw, sw, wa, wo, mask, fidx, fcnt, ftil, sidx, scnt, stil,
    ao, so,
    av_s, sv_s, as_s, ss_s, aw_s, sw_s, wa_s, wo_s, mask_s, fidx_s, fcnt_s, ft_s, sidx_s, scnt_s, st_s,
    wcat, wcat_t, ocat, ocat_t, mf,
    at, s1, adj, au,
    dx_f, dx_s, S_a, S_o, L_f, L_s, F, G, A_f, A_s, Cf, Cs, R_f, R_s,
    xl_a, xr_a, xl_o, xr_o, mine, from_lo, from_hi, halo_a, halo_o, as_p, fix, af_p,
    xl2_a, xr2_a, xl2_o, xr2_o, mine2, from_lo2, from_hi2, halo2_a, halo2_o,
    in_sem, send_sem, recv_sem,
):
    gx, gy = lax.axis_index("gx"), lax.axis_index("gy")
    right, left = lax.rem(gx + 1, nx), lax.rem(gx + nx - 1, nx)
    above, below = lax.rem(gy + 1, ny), lax.rem(gy + ny - 1, ny)
    to_right, to_left = (right, gy), (left, gy)
    to_above, to_below = (gx, above), (gx, below)
    last_a, last_o = air_x - 1, sea_x - 1

    def load_columns(src, dst, sem, count):
        for x in range(count):
            pltpu.make_async_copy(src.at[:, x, :], dst.at[x], in_sem.at[sem]).start()

    def loaded(dst, sem):
        pltpu.make_async_copy(dst, dst, in_sem.at[sem]).wait()

    def load(src, dst, sem):
        pltpu.make_async_copy(src, dst, in_sem.at[sem]).start()

    barrier = pltpu.get_barrier_semaphore()
    for device in (to_right, to_left, to_above, to_below):
        pl.semaphore_signal(barrier, inc=1, device_id=device, device_id_type=MESH)

    load(mask, mask_s, 0)
    load_columns(sv, sv_s, 1, sea_x)
    load_columns(av, av_s, 2, air_x)
    load(wa, wa_s, 3)
    load(wo, wo_s, 4)
    load(fidx.at[0], fidx_s, 5)
    load(fcnt, fcnt_s, 6)
    load(sidx.at[0], sidx_s, 7)
    load(scnt, scnt_s, 8)
    load_columns(asc, as_s, 9, air_x)
    load(ftil.at[0], ft_s, 10)
    load(stil.at[0], st_s, 11)
    load_columns(ssc, ss_s, 12, sea_x)
    load_columns(sw, sw_s, 13, sea_x)
    load_columns(aw, aw_s, 14, air_x)

    def remote(src, dst, k, device):
        return pltpu.make_async_remote_copy(
            src_ref=src, dst_ref=dst, send_sem=send_sem.at[k], recv_sem=recv_sem.at[k],
            device_id=device, device_id_type=MESH,
        )

    def start(*copies):
        for c in copies:
            c.start()
        return copies

    def wait(copies):
        for c in copies:
            c.wait()

    half = lax.broadcasted_iota(jnp.int32, (8, 128), 0) < 4

    def message(air_p, sea_p):
        lane = lane_of(sea_p)
        low = jnp.where(lane < 2 * air_x, air_p[:64], pltpu.roll(air_p[64:], 2 * air_x, 1))
        return jnp.where(lane < 4 * air_x, low, pltpu.roll(sea_p, 4 * air_x, 1))

    def open_messages(lo_ref, hi_ref, air_ref, sea_ref):
        lo = jnp.where(gy == 0, 0.0, lo_ref[...])
        hi = jnp.where(gy == ny - 1, 0.0, hi_ref[...])
        lane = lane_of(lo)
        air = jnp.where(
            lax.rem(lane, 2 * air_x) < air_x, pltpu.roll(lo, 128 - air_x, 1), pltpu.roll(hi, air_x, 1)
        )
        air_ref[...] = jnp.concatenate([air, pltpu.roll(air, 128 - 2 * air_x, 1)], axis=0)
        lo = pltpu.roll(lo, 128 - 4 * air_x - sea_x, 1)
        hi = pltpu.roll(hi, 128 - 4 * air_x + sea_x, 1)
        sea_ref[...] = jnp.where(lane < sea_x, lo, hi)

    def packed_air(ref):
        p = jnp.zeros((128, 128), f32)
        for x in range(air_x):
            p = put_ends(p, ref[x], x, air_x + x)
        return p

    def packed_sea(ref):
        p = jnp.zeros((64, 128), f32)
        for x in range(sea_x):
            p = put_ends(p, ref[x], x, sea_x + x)
        return p

    def phase_mask():
        loaded_mask = mask_s[...].astype(f32)
        mf[...] = loaded_mask
        for x in range(sea_x):
            sv_s[x] = loaded_mask[x:x + 1, :] * sv_s[x]

    def phase_pack():
        mine[...] = message(packed_air(av_s), packed_sea(sv_s))

    def phase_matrices():
        wcat[...] = split_cat(wa_s[...])
        wcat_t[...] = split_cat(wa_s[...].T)
        ocat[...] = split_cat(wo_s[...])
        ocat_t[...] = split_cat(wo_s[...].T)

    row_blocks = 32 * nx

    def places(idx_s, cnt_s, dx):
        own = gx * 32 + lax.broadcasted_iota(jnp.int32, (4, 32), 1)
        rel = idx_s[...] - own
        d = jnp.where(rel == 0, 0.0, jnp.where((rel == 1) | (rel == 1 - row_blocks), 1.0, -1.0))
        block = lax.broadcasted_iota(jnp.int32, (128, 32), 0) // 4
        pick = jnp.where(block == lax.broadcasted_iota(jnp.int32, (128, 32), 1), 1.0, 0.0)
        count = cnt_s[...].astype(f32)
        for k in range(4):
            dk = jnp.where(count > k, d[k:k + 1, :], 2.0)
            dx[k] = jnp.broadcast_to(jnp.sum(pick * dk, axis=1, keepdims=True), (128, 128))

    def phase_places():
        places(fidx_s, fcnt_s, dx_f)
        places(sidx_s, scnt_s, dx_s)

    def air_first(x, west, east):
        v = av_s[x]
        at[x] = col(wcat[...], as_s[x] * (GAIN * (v + west + east + lane_shifts(v))))

    def sea_first(x, west, east):
        v = sv_s[x]
        s1[x] = v + (GAIN * mf[x:x + 1, :]) * (west + east + lane_shifts(v) - 4.0 * v)

    def phase_air_first():
        for x in range(1, last_a):
            air_first(x, av_s[x - 1], av_s[x + 1])

    def phase_sea_first():
        for x in range(1, last_o):
            sea_first(x, sv_s[x - 1], sv_s[x + 1])

    def phase_as_pack():
        as_p[...] = packed_air(as_s)

    def phase_air_outer():
        air_first(0, xl_a[...], av_s[1])
        air_first(last_a, av_s[last_a - 1], xr_a[...])

    def phase_fix():
        fix[...] = col(wcat[...], as_p[...] * (GAIN * halo_a[...]))

    def air_ends(ref, x, rows=slice(None)):
        return ref[rows, x:x + 1], ref[rows, air_x + x:air_x + x + 1]

    def sea_ends(ref, x, rows=slice(None)):
        return ref[rows, x:x + 1], ref[rows, sea_x + x:sea_x + x + 1]

    def phase_air_surface():
        for x in range(air_x):
            low = rounded(with_ends(at[x, 120:128, :], *air_ends(fix, x, slice(120, 128))))
            S_a[8 + 8 * x:16 + 8 * x, :] = jnp.where(half, pltpu.roll(low[:, 0:128], 4, 0), low[:, 128:256])

    def sea_finish(x, v, rows):
        lo, hi = sea_ends(halo_o, x, rows)
        return with_ends(v, (GAIN * mf[x:x + 1, 0:1]) * lo, (GAIN * mf[x:x + 1, -1:]) * hi)

    def sea_outer(rows):
        for x, west, east in ((0, xl_o, sv_s.at[1]), (last_o, sv_s.at[last_o - 1], xr_o)):
            v = sv_s[x, rows, :]
            s1[x, rows, :] = v + (GAIN * mf[x:x + 1, :]) * (
                west[rows, :] + east[rows, :] + lane_shifts(v) - 4.0 * v
            )

    def to_slabs(top):
        out = []
        for q in range(2):
            a, b = top[:, 256 * q:256 * q + 128], top[:, 256 * q + 128:256 * q + 256]
            out.append(jnp.where(half, a, pltpu.roll(b, 4, 0)))
        return jnp.concatenate(out, axis=0)

    def phase_sea_surface():
        sea_outer(slice(0, 8))
        for x in range(sea_x):
            top = sea_finish(x, s1[x, 0:8, :], slice(0, 8))
            S_o[8 + 16 * x:24 + 16 * x, :] = to_slabs(rounded(top))

    def phase_sea_outer():
        sea_outer(slice(8, 64))

    def send_rims(src_hi, src_lo, k):
        return start(
            remote(src_hi.at[128:136], src_hi.at[0:8], k, to_right),
            remote(src_lo.at[8:16], src_lo.at[136:144], k + 1, to_left),
        )

    def gather_rows(S, dx, L, r0, r1):
        s_m, s_0, s_p = S[4 + r0:4 + r1], S[8 + r0:8 + r1], S[12 + r0:12 + r1]
        for k in range(4):
            d = dx[k, r0:r1]
            L[r0:r1, 128 * k:128 * k + 128] = jnp.where(
                d == 0.0, s_0, jnp.where(d == -1.0, s_m, jnp.where(d == 1.0, s_p, 0.0))
            )

    def pair_tiles(T, p):
        return jnp.concatenate(
            [jnp.concatenate([T[2 * p + a, k] for k in range(4)], axis=1) for a in range(2)], axis=0
        )

    def forward_pair(L, T, out, p):
        r = lax.dot_general(
            L[8 * p:8 * p + 8, :].astype(bf16), pair_tiles(T, p), (((1,), (1,)), ((), ())),
            preferred_element_type=f32,
        )
        out[8 * p:8 * p + 8, :] = jnp.where(half, r[:, 0:128], r[:, 128:256])

    def back_pair(A, T, dx, C, p):
        a = A[8 * p:8 * p + 8, :]
        lhs = jnp.concatenate([jnp.where(half, a, 0.0), jnp.where(half, 0.0, a)], axis=1)
        r = jnp.dot(lhs.astype(bf16), pair_tiles(T, p), preferred_element_type=f32)
        sums = [jnp.zeros((8, 128), f32) for _ in range(3)]
        for k in range(4):
            d = dx[k, 8 * p:8 * p + 8, :]
            c = r[:, 128 * k:128 * k + 128]
            for n in range(3):
                sums[n] = sums[n] + jnp.where(d == n - 1.0, c, 0.0)
        for n in range(3):
            C[n, 8 + 8 * p:16 + 8 * p, :] = sums[n]

    def phase_forward_skin():
        gather_rows(S_o, dx_s, L_s, 8, 120)
        for p in range(1, 15):
            forward_pair(L_s, st_s, G, p)

    def phase_forward_flux():
        gather_rows(S_a, dx_f, L_f, 8, 120)
        for p in range(1, 15):
            forward_pair(L_f, ft_s, F, p)

    def phase_forward_rims():
        for r0 in (0, 120):
            gather_rows(S_a, dx_f, L_f, r0, r0 + 8)
            gather_rows(S_o, dx_s, L_s, r0, r0 + 8)
        for p in (0, 15):
            forward_pair(L_f, ft_s, F, p)
            forward_pair(L_s, st_s, G, p)

    def sea_top(ref, x):
        parts = []
        for q in range(2):
            slab = ref[16 * x + 8 * q:16 * x + 8 * q + 8, :]
            parts.append(jnp.where(half, slab, 0.0))
            parts.append(jnp.where(half, pltpu.roll(slab, 4, 0), 0.0))
        return jnp.concatenate(parts, axis=1)

    def sea_columns(x):
        m = mf[x:x + 1, :]
        one = sea_finish(x, s1[x], slice(None))
        two = jnp.concatenate([one[0:8] + m * sea_top(F, x), one[8:]], axis=0)
        three = col(ocat[...], ss_s[x] * two)
        back = m * (ss_s[x] * col(ocat_t[...], m * (sw_s[x] * three)))
        adj[x] = back
        A_f[16 * x:16 * x + 16, :] = to_slabs(rounded(back[0:8]))

    def phase_sea_columns_outer():
        sea_columns(0)
        sea_columns(last_o)

    def phase_sea_columns():
        for x in range(1, last_o):
            sea_columns(x)

    def air_low(ref, x):
        slab = ref[8 * x:8 * x + 8, :]
        return jnp.concatenate(
            [jnp.where(half, 0.0, pltpu.roll(slab, 4, 0)), jnp.where(half, 0.0, slab)], axis=1
        )

    def air_forcing(x):
        two = with_ends(at[x], *air_ends(fix, x))
        three = jnp.concatenate([two[0:120], two[120:128] + air_low(G, x)], axis=0)
        forcing = aw_s[x] * three
        at[x] = forcing
        low = rounded(forcing[120:128])
        A_s[8 * x:8 * x + 8, :] = jnp.where(half, pltpu.roll(low[:, 0:128], 4, 0), low[:, 128:256])

    def phase_air_forcing_outer():
        air_forcing(0)
        air_forcing(last_a)

    def phase_air_forcing():
        for x in range(1, last_a):
            air_forcing(x)

    def phase_air_pack():
        af_p[...] = packed_air(at)

    def phase_back_flux_rims():
        for p in (0, 15):
            back_pair(A_f, ft_s, dx_f, Cf, p)

    def phase_back_skin_rims():
        for p in (0, 15):
            back_pair(A_s, st_s, dx_s, Cs, p)

    def phase_back_flux():
        for p in range(1, 15):
            back_pair(A_f, ft_s, dx_f, Cf, p)

    def phase_back_skin():
        for p in range(1, 15):
            back_pair(A_s, st_s, dx_s, Cs, p)

    def arrived(C, R, r0, r1):
        R[r0:r1, :] = C[1, r0 + 8:r1 + 8] + C[0, r0 + 12:r1 + 12] + C[2, r0 + 4:r1 + 4]

    def sea_upper(xs):
        for x in xs:
            adj[x, 0:8, :] = adj[x, 0:8, :] + mf[x:x + 1, :] * sea_top(R_s, x)

    def air_lower(xs):
        p = af_p[120:128, :]
        for x in xs:
            low = at[x, 120:128, :] + air_low(R_f, x)
            at[x, 120:128, :] = low
            p = put_ends(p, low, x, air_x + x)
        af_p[120:128, :] = p

    def phase_sea_upper():
        arrived(Cs, R_s, 16, 112)
        sea_upper(range(1, last_o))

    def phase_air_lower():
        arrived(Cf, R_f, 8, 120)
        air_lower(range(1, last_a))

    def phase_sea_upper_outer():
        arrived(Cs, R_s, 0, 16)
        arrived(Cs, R_s, 112, 128)
        sea_upper((0, last_o))

    def phase_air_lower_outer():
        arrived(Cf, R_f, 0, 8)
        arrived(Cf, R_f, 120, 128)
        air_lower((0, last_a))

    def phase_pack_last():
        air_p = as_p[...] * col(wcat_t[...], af_p[...])
        mine2[...] = message(air_p, packed_sea(adj))

    def air_upper(x):
        au[x] = as_s[x] * col(wcat_t[...], at[x])

    def phase_air_upper_outer():
        air_upper(0)
        air_upper(last_a)

    def phase_air_upper():
        for x in range(1, last_a):
            air_upper(x)

    def sea_last(x, west, east):
        z = adj[x]
        so[x] = z + (GAIN * mf[x:x + 1, :]) * (west + east + lane_shifts(z) - 4.0 * z)

    def air_last(x, west, east):
        v = au[x]
        ao[x] = GAIN * (v + west + east + lane_shifts(v))

    def phase_last():
        for x in range(1, last_o):
            sea_last(x, adj[x - 1], adj[x + 1])
        for x in range(1, last_a):
            air_last(x, au[x - 1], au[x + 1])

    def last_ends(sea_xs, air_xs):
        for x in sea_xs:
            lo, hi = sea_ends(halo2_o, x)
            so[x] = with_ends(so[x], (GAIN * mf[x:x + 1, 0:1]) * lo, (GAIN * mf[x:x + 1, -1:]) * hi)
        for x in air_xs:
            lo, hi = air_ends(halo2_a, x)
            ao[x] = with_ends(ao[x], GAIN * lo, GAIN * hi)

    def last_outer():
        sea_last(0, xl2_o[...], adj[1])
        sea_last(last_o, adj[last_o - 1], xr2_o[...])
        air_last(0, xl2_a[...], au[1])
        air_last(last_a, au[last_a - 1], xr2_a[...])
        last_ends((0, last_o), (0, last_a))

    pl.semaphore_wait(barrier, 4)
    halo_a1 = start(
        remote(av.at[:, last_a, :], xl_a, 0, to_right),
        remote(av.at[:, 0, :], xr_a, 1, to_left),
    )
    loaded(mask_s, 0)
    loaded(sv_s, 1)
    phase_mask()
    halo_o1 = start(
        remote(sv_s.at[last_o, 0:8], xl_o.at[0:8], 2, to_right),
        remote(sv_s.at[0, 0:8], xr_o.at[0:8], 3, to_left),
    )
    loaded(av_s, 2)
    phase_pack()
    halo_y1 = start(remote(mine, from_lo, 4, to_above), remote(mine, from_hi, 5, to_below))
    halo_o1_rest = start(
        remote(sv_s.at[last_o, 8:64], xl_o.at[8:64], 14, to_right),
        remote(sv_s.at[0, 8:64], xr_o.at[8:64], 15, to_left),
    )
    loaded(wa_s, 3)
    loaded(wo_s, 4)
    phase_matrices()
    loaded(fidx_s, 5)
    loaded(fcnt_s, 6)
    loaded(sidx_s, 7)
    loaded(scnt_s, 8)
    phase_places()
    phase_sea_first()
    loaded(as_s, 9)
    phase_air_first()
    phase_as_pack()

    wait(halo_y1)
    open_messages(from_lo, from_hi, halo_a, halo_o)
    phase_fix()
    wait(halo_o1)
    phase_sea_surface()
    rim_o = send_rims(S_o, S_o, 8)
    wait(halo_a1)
    phase_air_outer()
    phase_air_surface()
    rim_a = send_rims(S_a, S_a, 6)

    loaded(st_s, 11)
    phase_forward_skin()
    loaded(ft_s, 10)
    phase_forward_flux()
    loaded(ss_s, 12)
    loaded(sw_s, 13)
    phase_sea_columns()
    wait(rim_a)
    wait(rim_o)
    phase_forward_rims()
    wait(halo_o1_rest)
    phase_sea_outer()
    phase_sea_columns_outer()
    loaded(aw_s, 14)
    phase_air_forcing_outer()
    phase_back_flux_rims()
    phase_back_skin_rims()
    rim_f = send_rims(Cf.at[2], Cf.at[0], 10)
    rim_s = send_rims(Cs.at[2], Cs.at[0], 12)
    halo_o2_rest = start(
        remote(adj.at[last_o, 8:64], xl2_o.at[8:64], 16, to_right),
        remote(adj.at[0, 8:64], xr2_o.at[8:64], 17, to_left),
    )
    phase_air_forcing()
    phase_air_pack()
    phase_back_flux()
    phase_air_lower()
    phase_back_skin()
    phase_sea_upper()
    phase_air_upper()

    wait(rim_f)
    phase_air_lower_outer()
    phase_air_upper_outer()
    halo_a2 = start(remote(au.at[last_a], xl2_a, 18, to_right), remote(au.at[0], xr2_a, 19, to_left))
    wait(rim_s)
    phase_sea_upper_outer()
    halo_o2 = start(
        remote(adj.at[last_o, 0:8], xl2_o.at[0:8], 20, to_right),
        remote(adj.at[0, 0:8], xr2_o.at[0:8], 21, to_left),
    )
    phase_pack_last()
    halo_y2 = start(remote(mine2, from_lo2, 22, to_above), remote(mine2, from_hi2, 23, to_below))
    phase_last()
    wait(halo_y2)
    open_messages(from_lo2, from_hi2, halo2_a, halo2_o)
    last_ends(range(1, last_o), range(1, last_a))
    wait(halo_o2_rest)
    wait(halo_o2)
    wait(halo_a2)
    last_outer()


def deliver(a, o, aout, sout, sem):
    for x in range(a.shape[0]):
        pltpu.make_async_copy(a.at[x], aout.at[:, x, :], sem.at[0]).start()
    for x in range(o.shape[0]):
        pltpu.make_async_copy(o.at[x], sout.at[:, x, :], sem.at[1]).start()
    pltpu.make_async_copy(a, a, sem.at[0]).wait()
    pltpu.make_async_copy(o, o, sem.at[1]).wait()


def shards(*args, nx, ny):
    av, sv = args[0], args[1]
    args = [a.transpose(0, 2, 1) if n in (9, 12) else a for n, a in enumerate(args)]
    args = [pltpu.with_memory_space_constraint(a, pltpu.HBM) for a in args]
    levels, air_x, air_y = av.shape
    sea_levels, sea_x, sea_y = sv.shape
    V = pltpu.VMEM
    air = V((air_x, levels, air_y), f32)
    sea = V((sea_x, sea_levels, sea_y), f32)
    blk = V((128, 128), f32)
    ext = V((144, 128), f32)
    rowa, rowo, pack = V((levels, air_y), f32), V((sea_levels, sea_y), f32), V((64, 128), f32)
    tiles = V((32, 4, 128, 128), bf16)
    idx, cnt = V((4, 32), jnp.int32), V((1, 32), jnp.int32)
    wcat = V((2 * levels, 2 * levels), bf16)
    ocat = V((2 * sea_levels, 2 * sea_levels), bf16)
    dx = V((4, 128, 128), f32)
    cterm = V((3, 144, 128), f32)
    dma = pltpu.SemaphoreType.DMA
    scratch = [
        air, sea, air, sea, air, sea, V((levels, levels), f32), V((sea_levels, sea_levels), f32),
        V((sea_x, sea_y), jnp.int32), idx, cnt, tiles, idx, cnt, tiles,
        wcat, wcat, ocat, ocat, V((sea_x, sea_y), f32),
        air, sea, sea, air,
        dx, dx, ext, ext, V((128, 512), f32), V((128, 512), f32), blk, blk, blk, blk, cterm, cterm, blk, blk,
        rowa, rowa, rowo, rowo, pack, pack, pack, blk, pack, blk, blk, blk,
        rowa, rowa, rowo, rowo, pack, pack, pack, blk, pack,
        dma((15,)), dma((24,)), dma((24,)),
    ]
    anywhere = pl.BlockSpec(memory_space=pl.ANY)
    outs = (jax.ShapeDtypeStruct(av.shape, f32), jax.ShapeDtypeStruct(sv.shape, f32))
    held = pl.pallas_call(
        functools.partial(kernel, nx, ny, air_x, sea_x),
        out_shape=(air, sea),
        in_specs=[pl.BlockSpec(memory_space=pltpu.HBM)] * 15,
        out_specs=[pl.BlockSpec(memory_space=pltpu.VMEM)] * 2,
        scratch_shapes=scratch,
        compiler_params=pltpu.CompilerParams(
            collective_id=0, has_side_effects=True, vmem_limit_bytes=44 * 1024 * 1024
        ),
        cost_estimate=pl.CostEstimate(flops=4_000_000_000, bytes_accessed=21_000_000, transcendentals=0),
    )(*args)
    return pl.pallas_call(
        deliver,
        out_shape=outs,
        in_specs=[anywhere] * 2,
        out_specs=[pl.BlockSpec(memory_space=pltpu.HBM)] * 2,
        scratch_shapes=[dma((2,))],
        compiler_params=pltpu.CompilerParams(vmem_limit_bytes=1024 * 1024),
    )(*held)


def solution(mesh):
    grid = P(None, "gx", "gy")
    index, count, tiles = P("gy", "gx", None), P("gy", "gx"), P("gy", "gx", None, None, None)
    return jax.shard_map(
        functools.partial(shards, nx=mesh.shape["gx"], ny=mesh.shape["gy"]),
        mesh=mesh,
        in_specs=(grid,) * 6 + (P(), P(), P("gx", "gy"), index, count, tiles, index, count, tiles),
        out_specs=(grid, grid),
        check_vma=False,
    )
```

time: 42 us -> 33.5 us (0.80)
  Pallas kernels: 37.1 us -> 32.6 us
  local copies, waits for them, and re-layouts: 4.14 us -> 0 us
    pallas_call x1, Pallas kernels: 37.1 us -> 31 us  [shards(): pl.pallas_call(functools.partial(kernel, nx, ny, air_x, sea_x), out_shape...]
    unnamed x4 -> x0, local copies, waits for them, and re-layouts: 4.14 us -> none
    pallas_call x0 -> x1, Pallas kernels: none -> 1.66 us  [shards(): pl.pallas_call(deliver, out_shape=outs, in_specs=[anywhere] * 2, out_spec...]
where the time goes in v3:
time: 33.5 us; the launch traced here: 33.3 us
  Pallas kernels  32.6 us (97%)
  between operations  0.64 us (2%)
    pallas_call x1, Pallas kernels, shards(): pl.pallas_call(functools.partial(kernel, nx, ny, air_x, sea_x), out_shape...  31 us
    pallas_call x1, Pallas kernels, shards(): pl.pallas_call(deliver, out_shape=outs, in_specs=[anywhere] * 2, out_spec...  1.66 us

profile of v3, /device:TPU:0, one launch (start us, length us, event | category | flops | bytes accessed | tf_op | source)
XLA Modules:
  0.0 33.3 jit_solution(9981139008199197677)
XLA Ops:
  0.6 31.0 %shard_map.158 = (f32[16,128,256]{2,1,0:T(8,128)S(1)}, f32[8,64,512]{2,1,0:T(8,128)S(1)}) custom-call(f32[128,16,256]{2,1,0:T(8,128)} %av.1, f32[64,8,512]{2,1,0:T(8,128)} %sv.1, f32[128,16,256]{2,1,0:T(8,128)} %asc.1, f32[64,8,512]{2,1,0:T(8,128)} %ssc.1, f32[128,16,256]{2,1,0:T(8,128)} %aw.1, f32[64,8,512]{2,1,0:T(8,128)} %sw.1, f32[128,128]{1,0:T(8,128)} %wa.1, ...), custom_call_target="tpu_custom_call" | custom-call | flops 4000000000 | bytes 21000000 | tf_op jit(solution)/shard_map/pallas_call | solution.py:590
  31.6 1.7 %shard_map.159 = (f32[128,16,256]{2,1,0:T(8,128)}, f32[64,8,512]{2,1,0:T(8,128)}) custom-call(f32[16,128,256]{2,1,0:T(8,128)S(1)} %get-tuple-element.4.a, f32[8,64,512]{2,1,0:T(8,128)S(1)} %get-tuple-element.5.o), custom_call_target="tpu_custom_call" | custom-call | tf_op jit(solution)/shard_map/pallas_call | solution.py:601

commit v4 on v3

--- a/solution.py
+++ b/solution.py
@@ -70,6 +70,7 @@
     dx_f, dx_s, S_a, S_o, L_f, L_s, F, G, A_f, A_s, Cf, Cs, R_f, R_s,
     xl_a, xr_a, xl_o, xr_o, mine, from_lo, from_hi, halo_a, halo_o, as_p, fix, af_p,
     xl2_a, xr2_a, xl2_o, xr2_o, mine2, from_lo2, from_hi2, halo2_a, halo2_o,
+    own_l, own_r, top_l, top_r, as_l, as_r, m_l, m_r, df_lo, df_hi, ds_lo, ds_hi,
     in_sem, send_sem, recv_sem,
 ):
     gx, gy = lax.axis_index("gx"), lax.axis_index("gy")
@@ -77,6 +78,7 @@
     above, below = lax.rem(gy + 1, ny), lax.rem(gy + ny - 1, ny)
     to_right, to_left = (right, gy), (left, gy)
     to_above, to_below = (gx, above), (gx, below)
+    to_left_above, to_right_below = (left, above), (right, below)
     last_a, last_o = air_x - 1, sea_x - 1
 
     def load_columns(src, dst, sem, count):
@@ -90,7 +92,7 @@
         pltpu.make_async_copy(src, dst, in_sem.at[sem]).start()
 
     barrier = pltpu.get_barrier_semaphore()
-    for device in (to_right, to_left, to_above, to_below):
+    for device in (to_right, to_left, to_above, to_below, to_left_above, to_right_below):
         pl.semaphore_signal(barrier, inc=1, device_id=device, device_id_type=MESH)
 
     load(mask, mask_s, 0)
@@ -359,27 +361,23 @@
         af_p[...] = packed_air(at)
 
     def phase_back_flux_rims():
-        for p in (0, 15):
+        for p in (0, 1, 14, 15):
             back_pair(A_f, ft_s, dx_f, Cf, p)
 
-    def phase_back_skin_rims():
-        for p in (0, 15):
+    def phase_back_flux():
+        for p in range(2, 14):
+            back_pair(A_f, ft_s, dx_f, Cf, p)
+
+    def phase_back_skin():
+        for p in range(16):
             back_pair(A_s, st_s, dx_s, Cs, p)
 
-    def phase_back_flux():
-        for p in range(1, 15):
-            back_pair(A_f, ft_s, dx_f, Cf, p)
-
-    def phase_back_skin():
-        for p in range(1, 15):
-            back_pair(A_s, st_s, dx_s, Cs, p)
-
-    def arrived(C, R, r0, r1):
+    def own_terms(C, R, r0, r1):
         R[r0:r1, :] = C[1, r0 + 8:r1 + 8] + C[0, r0 + 12:r1 + 12] + C[2, r0 + 4:r1 + 4]
 
-    def sea_upper(xs):
-        for x in xs:
-            adj[x, 0:8, :] = adj[x, 0:8, :] + mf[x:x + 1, :] * sea_top(R_s, x)
+    def own_terms_ends(C, R):
+        R[0:8, :] = C[1, 8:16] + C[0, 12:20] + jnp.where(half, 0.0, pltpu.roll(C[2, 8:16], 4, 0))
+        R[120:128, :] = C[1, 128:136] + C[2, 124:132] + jnp.where(half, pltpu.roll(C[0, 128:136], 4, 0), 0.0)
 
     def air_lower(xs):
         p = af_p[120:128, :]
@@ -389,27 +387,76 @@
             p = put_ends(p, low, x, air_x + x)
         af_p[120:128, :] = p
 
+    def phase_own_outer():
+        own_terms_ends(Cf, R_f)
+        air_lower((0, last_a))
+        own_l[...] = as_s[0] * col(wcat_t[...], at[0])
+        own_r[...] = as_s[last_a] * col(wcat_t[...], at[last_a])
+
+    def phase_air_lower():
+        own_terms(Cf, R_f, 8, 120)
+        air_lower(range(1, last_a))
+
     def phase_sea_upper():
-        arrived(Cs, R_s, 16, 112)
-        sea_upper(range(1, last_o))
-
-    def phase_air_lower():
-        arrived(Cf, R_f, 8, 120)
-        air_lower(range(1, last_a))
-
-    def phase_sea_upper_outer():
-        arrived(Cs, R_s, 0, 16)
-        arrived(Cs, R_s, 112, 128)
-        sea_upper((0, last_o))
-
-    def phase_air_lower_outer():
-        arrived(Cf, R_f, 0, 8)
-        arrived(Cf, R_f, 120, 128)
-        air_lower((0, last_a))
+        own_terms(Cs, R_s, 8, 120)
+        own_terms_ends(Cs, R_s)
+        for x in range(sea_x):
+            adj[x, 0:8, :] = adj[x, 0:8, :] + mf[x:x + 1, :] * sea_top(R_s, x)
+        top_l[...] = adj[0, 0:8, :]
+        top_r[...] = adj[last_o, 0:8, :]
+
+    zero_rows = jnp.zeros((120, 128), f32)
+
+    def low_rows(slab, first):
+        rows = pltpu.roll(slab, 4, 0) if first else slab
+        return jnp.concatenate([zero_rows, jnp.where(half, 0.0, rows)], axis=0)
+
+    def phase_beside():
+        terms = jnp.concatenate([low_rows(Cf[0, 8:16], True), low_rows(Cf[2, 128:136], False)], axis=1)
+        r = col(wcat_t[...], terms)
+        as_l[...] = as_l[...] * r[:, :128]
+        as_r[...] = as_r[...] * r[:, 128:]
+
+    def phase_rims_arrived():
+        at[0, 120:128, 0:128] = at[0, 120:128, 0:128] + jnp.where(half, 0.0, Cf[2, 0:8])
+        at[last_a, 120:128, 128:] = at[last_a, 120:128, 128:] + jnp.where(half, 0.0, pltpu.roll(Cf[0, 136:144], 4, 0))
+        first = jnp.where(half, pltpu.roll(Cs[2, 0:8], 4, 0), 0.0)
+        adj[0, 0:8, 0:128] = adj[0, 0:8, 0:128] + mf[0:1, 0:128] * first
+        final = jnp.where(half, Cs[0, 136:144], 0.0)
+        adj[last_o, 0:8, -128:] = adj[last_o, 0:8, -128:] + mf[last_o:last_o + 1, -128:] * final
+
+    def phase_diagonal():
+        lo = jnp.where(gy == 0, 0.0, 1.0)
+        hi = jnp.where(gy == ny - 1, 0.0, 1.0)
+        lane = lane_of(zero_rows)[0:8]
+        t_lo = lo * jnp.where(half, 0.0, pltpu.roll(df_lo[...], 4, 0))
+        t_hi = hi * jnp.where(half, 0.0, df_hi[...])
+        tile = jnp.where(lane == last_a, t_lo[:, 127:128], jnp.where(lane == air_x, t_hi[:, 0:1], 0.0))
+        r = col(wcat_t[...], jnp.concatenate([zero_rows, tile], axis=0))
+        scale = jnp.concatenate([from_lo2[:, 81:82], from_lo2[:, 83:84]], axis=0)
+        scale_hi = jnp.concatenate([from_hi2[:, 80:81], from_hi2[:, 82:83]], axis=0)
+        wide = lane_of(r)
+        halo2_a[...] = halo2_a[...] + r * jnp.where(wide == last_a, scale, jnp.where(wide == air_x, scale_hi, 0.0))
+        o_lo = lo * jnp.where(half, ds_lo[...], 0.0)
+        o_hi = hi * jnp.where(half, pltpu.roll(ds_hi[...], 4, 0), 0.0)
+        o_lo = o_lo[:, 127:128] * from_lo2[0:8, 85:86]
+        o_hi = o_hi[:, 0:1] * from_hi2[0:8, 84:85]
+        halo2_o[0:8, :] = halo2_o[0:8, :] + jnp.where(
+            lane == last_o, o_lo, jnp.where(lane == sea_x, o_hi, 0.0)
+        )
 
     def phase_pack_last():
         air_p = as_p[...] * col(wcat_t[...], af_p[...])
-        mine2[...] = message(air_p, packed_sea(adj))
+        m = message(air_p, packed_sea(adj))
+        lane = lane_of(m)
+        first, final = as_p[:, 0:1], as_p[:, air_x + last_a:air_x + last_a + 1]
+        extra = (
+            (80, first[:64]), (82, first[64:]), (81, final[:64]), (83, final[64:]),
+            (84, mf[0:1, 0:1]), (85, mf[last_o:last_o + 1, -1:]),
+        )
+        for n, v in extra:
+            m = jnp.where(lane == n, v, m)
+        mine2[...] = m
 
     def air_upper(x):
         au[x] = as_s[x] * col(wcat_t[...], at[x])
@@ -431,9 +478,15 @@
         ao[x] = GAIN * (v + west + east + lane_shifts(v))
 
     def phase_last():
-        for x in range(1, last_o):
+        for x in range(2, last_o - 1):
             sea_last(x, adj[x - 1], adj[x + 1])
-        for x in range(1, last_a):
+        for x in range(2, last_a - 1):
+            air_last(x, au[x - 1], au[x + 1])
+
+    def phase_last_next():
+        for x in (1, last_o - 1):
+            sea_last(x, adj[x - 1], adj[x + 1])
+        for x in (1, last_a - 1):
             air_last(x, au[x - 1], au[x + 1])
 
     def last_ends(sea_xs, air_xs):
@@ -445,13 +498,17 @@
             ao[x] = with_ends(ao[x], GAIN * lo, GAIN * hi)
 
     def last_outer():
+        xl2_o[0:8, -128:] = xl2_o[0:8, -128:] + m_l[last_o:last_o + 1, :] * jnp.where(half, Cs[0, 8:16], 0.0)
+        xr2_o[0:8, 0:128] = xr2_o[0:8, 0:128] + m_r[0:1, :] * jnp.where(half, pltpu.roll(Cs[2, 128:136], 4, 0), 0.0)
+        xl2_a[:, 128:] = xl2_a[:, 128:] + as_l[...]
+        xr2_a[:, 0:128] = xr2_a[:, 0:128] + as_r[...]
         sea_last(0, xl2_o[...], adj[1])
         sea_last(last_o, adj[last_o - 1], xr2_o[...])
         air_last(0, xl2_a[...], au[1])
         air_last(last_a, au[last_a - 1], xr2_a[...])
         last_ends((0, last_o), (0, last_a))
 
-    pl.semaphore_wait(barrier, 4)
+    pl.semaphore_wait(barrier, 6)
     halo_a1 = start(
         remote(av.at[:, last_a, :], xl_a, 0, to_right),
         remote(av.at[:, 0, :], xr_a, 1, to_left),
@@ -498,48 +555,65 @@
     phase_forward_skin()
     loaded(ft_s, 10)
     phase_forward_flux()
+    beside = start(
+        remote(asc.at[:, last_a, 128:256], as_l, 24, to_right),
+        remote(asc.at[:, 0, 0:128], as_r, 25, to_left),
+        remote(mf.at[:, mf.shape[1] - 128:], m_l, 26, to_right),
+        remote(mf.at[:, 0:128], m_r, 27, to_left),
+    )
     loaded(ss_s, 12)
     loaded(sw_s, 13)
     phase_sea_columns()
+    loaded(aw_s, 14)
+    phase_air_forcing()
     wait(rim_a)
     wait(rim_o)
     phase_forward_rims()
     wait(halo_o1_rest)
     phase_sea_outer()
     phase_sea_columns_outer()
-    loaded(aw_s, 14)
-    phase_air_forcing_outer()
-    phase_back_flux_rims()
-    phase_back_skin_rims()
-    rim_f = send_rims(Cf.at[2], Cf.at[0], 10)
-    rim_s = send_rims(Cs.at[2], Cs.at[0], 12)
     halo_o2_rest = start(
         remote(adj.at[last_o, 8:64], xl2_o.at[8:64], 16, to_right),
         remote(adj.at[0, 8:64], xr2_o.at[8:64], 17, to_left),
     )
-    phase_air_forcing()
+    phase_air_forcing_outer()
+    phase_back_flux_rims()
+    rim_f = send_rims(Cf.at[2], Cf.at[0], 10)
+    diagonal = start(
+        remote(Cf.at[0, 8:16], df_lo, 28, to_left_above),
+        remote(Cf.at[2, 128:136], df_hi, 29, to_right_below),
+    )
     phase_air_pack()
+    phase_own_outer()
+    halo_a2 = start(remote(own_r, xl2_a, 18, to_right), remote(own_l, xr2_a, 19, to_left))
+    phase_back_skin()
+    rim_s = send_rims(Cs.at[2], Cs.at[0], 12)
+    diagonal += start(
+        remote(Cs.at[0, 8:16], ds_lo, 30, to_left_above),
+        remote(Cs.at[2, 128:136], ds_hi, 31, to_right_below),
+    )
+    phase_sea_upper()
+    halo_o2 = start(
+        remote(top_r, xl2_o.at[0:8], 20, to_right),
+        remote(top_l, xr2_o.at[0:8], 21, to_left),
+    )
     phase_back_flux()
     phase_air_lower()
-    phase_back_skin()
-    phase_sea_upper()
-    phase_air_upper()
-
-    wait(rim_f)
-    phase_air_lower_outer()
-    phase_air_upper_outer()
-    halo_a2 = start(remote(au.at[last_a], xl2_a, 18, to_right), remote(au.at[0], xr2_a, 19, to_left))
-    wait(rim_s)
-    phase_sea_upper_outer()
-    halo_o2 = start(
-        remote(adj.at[last_o, 0:8], xl2_o.at[0:8], 20, to_right),
-        remote(adj.at[0, 0:8], xr2_o.at[0:8], 21, to_left),
-    )
     phase_pack_last()
     halo_y2 = start(remote(mine2, from_lo2, 22, to_above), remote(mine2, from_hi2, 23, to_below))
+    phase_air_upper()
+    wait(beside)
+    phase_beside()
     phase_last()
+    wait(rim_f)
+    wait(rim_s)
+    phase_rims_arrived()
+    phase_air_upper_outer()
+    phase_last_next()
     wait(halo_y2)
     open_messages(from_lo2, from_hi2, halo2_a, halo2_o)
+    wait(diagonal)
+    phase_diagonal()
     last_ends(range(1, last_o), range(1, last_a))
     wait(halo_o2_rest)
     wait(halo_o2)
@@ -574,6 +648,7 @@
     ocat = V((2 * sea_levels, 2 * sea_levels), bf16)
     dx = V((4, 128, 128), f32)
     cterm = V((3, 144, 128), f32)
+    tile = V((8, 128), f32)
     dma = pltpu.SemaphoreType.DMA
     scratch = [
         air, sea, air, sea, air, sea, V((levels, levels), f32), V((sea_levels, sea_levels), f32),
@@ -583,7 +658,8 @@
         dx, dx, ext, ext, V((128, 512), f32), V((128, 512), f32), blk, blk, blk, blk, cterm, cterm, blk, blk,
         rowa, rowa, rowo, rowo, pack, pack, pack, blk, pack, blk, blk, blk,
         rowa, rowa, rowo, rowo, pack, pack, pack, blk, pack,
-        dma((15,)), dma((24,)), dma((24,)),
+        rowa, rowa, V((8, sea_y), f32), V((8, sea_y), f32), blk, blk, tile, tile, tile, tile, tile, tile,
+        dma((15,)), dma((32,)), dma((32,)),
     ]
     anywhere = pl.BlockSpec(memory_space=pl.ANY)
     outs = (jax.ShapeDtypeStruct(av.shape, f32), jax.ShapeDtypeStruct(sv.shape, f32))

time: 33.5 us -> 32.4 us (0.967)
  Pallas kernels: 32.6 us -> 31.6 us
    pallas_call x1, Pallas kernels: 31 us -> 29.9 us  [shards(): pl.pallas_call(functools.partial(kernel, nx, ny, air_x, sea_x), out_shape...]
where the time goes in v4:
time: 32.4 us; the launch traced here: 32.2 us
  Pallas kernels  31.6 us (98%)
  between operations  0.64 us (2%)
    pallas_call x1, Pallas kernels, shards(): pl.pallas_call(functools.partial(kernel, nx, ny, air_x, sea_x), out_shape...  29.9 us
    pallas_call x1, Pallas kernels, shards(): pl.pallas_call(deliver, out_shape=outs, in_specs=[anywhere] * 2, out_spec...  1.66 us

profile of v4, /device:TPU:0, one launch (start us, length us, event | category | flops | bytes accessed | tf_op | source)
XLA Modules:
  0.0 32.2 jit_solution(15802932447039122251)
XLA Ops:
  0.6 29.9 %shard_map.158 = (f32[16,128,256]{2,1,0:T(8,128)S(1)}, f32[8,64,512]{2,1,0:T(8,128)S(1)}) custom-call(f32[128,16,256]{2,1,0:T(8,128)} %av.1, f32[64,8,512]{2,1,0:T(8,128)} %sv.1, f32[128,16,256]{2,1,0:T(8,128)} %asc.1, f32[64,8,512]{2,1,0:T(8,128)} %ssc.1, f32[128,16,256]{2,1,0:T(8,128)} %aw.1, f32[64,8,512]{2,1,0:T(8,128)} %sw.1, f32[128,128]{1,0:T(8,128)} %wa.1, ...), custom_call_target="tpu_custom_call" | custom-call | flops 4000000000 | bytes 21000000 | tf_op jit(solution)/shard_map/pallas_call | solution.py:666
  30.6 1.7 %shard_map.159 = (f32[128,16,256]{2,1,0:T(8,128)}, f32[64,8,512]{2,1,0:T(8,128)}) custom-call(f32[16,128,256]{2,1,0:T(8,128)S(1)} %get-tuple-element.4.a, f32[8,64,512]{2,1,0:T(8,128)S(1)} %get-tuple-element.5.o), custom_call_target="tpu_custom_call" | custom-call | tf_op jit(solution)/shard_map/pallas_call | solution.py:677

commit v5 on v4

--- a/solution.py
+++ b/solution.py
@@ -70,7 +70,7 @@
     dx_f, dx_s, S_a, S_o, L_f, L_s, F, G, A_f, A_s, Cf, Cs, R_f, R_s,
     xl_a, xr_a, xl_o, xr_o, mine, from_lo, from_hi, halo_a, halo_o, as_p, fix, af_p,
     xl2_a, xr2_a, xl2_o, xr2_o, mine2, from_lo2, from_hi2, halo2_a, halo2_o,
-    own_l, own_r, top_l, top_r, as_l, as_r, m_l, m_r, df_lo, df_hi, ds_lo, ds_hi,
+    rim_lo, rim_hi, own_l, own_r, top_l, top_r, as_l, as_r, m_l, m_r, df_lo, df_hi, ds_lo, ds_hi,
     in_sem, send_sem, recv_sem,
 ):
     gx, gy = lax.axis_index("gx"), lax.axis_index("gy")
@@ -208,9 +208,23 @@
     def phase_as_pack():
         as_p[...] = packed_air(as_s)
 
+    def outer_halves(first, final):
+        fields = []
+        for x, west, east, lanes in ((0, xl_a, av_s.at[1], first), (last_a, av_s.at[last_a - 1], xr_a, final)):
+            v = av_s[x]
+            near = v + lane_shifts(v)
+            fields.append(as_s[x, :, lanes] * (GAIN * (near[:, lanes] + west[:, lanes] + east[:, lanes])))
+        r = col(wcat[...], jnp.concatenate(fields, axis=1))
+        at[0, :, first] = r[:, 0:128]
+        at[last_a, :, final] = r[:, 128:256]
+
+    low_half, high_half = slice(0, 128), slice(128, 256)
+
+    def phase_air_ends():
+        outer_halves(low_half, high_half)
+
     def phase_air_outer():
-        air_first(0, xl_a[...], av_s[1])
-        air_first(last_a, av_s[last_a - 1], xr_a[...])
+        outer_halves(high_half, low_half)
 
     def phase_fix():
         fix[...] = col(wcat[...], as_p[...] * (GAIN * halo_a[...]))
@@ -220,6 +234,13 @@
 
     def sea_ends(ref, x, rows=slice(None)):
         return ref[rows, x:x + 1], ref[rows, sea_x + x:sea_x + x + 1]
+
+    def phase_air_rims():
+        lane = lane_of(fix[120:128, :])
+        a = at[0, 120:128, 0:128] + jnp.where(lane == 0, fix[120:128, 0:1], 0.0)
+        b = at[last_a, 120:128, 128:256] + jnp.where(lane == 127, fix[120:128, 2 * air_x - 1:2 * air_x], 0.0)
+        rim_lo[...] = jnp.where(half, pltpu.roll(rounded(a), 4, 0), 0.0)
+        rim_hi[...] = jnp.where(half, 0.0, rounded(b))
 
     def phase_air_surface():
         for x in range(air_x):
@@ -358,7 +379,14 @@
             air_forcing(x)
 
     def phase_air_pack():
-        af_p[...] = packed_air(at)
+        p = jnp.zeros((128, 128), f32)
+        for x in range(1, last_a):
+            p = put_ends(p, at[x], x, air_x + x)
+        af_p[...] = p
+
+    def phase_air_pack_outer():
+        p = put_ends(af_p[...], at[0], 0, air_x)
+        af_p[...] = put_ends(p, at[last_a], last_a, air_x + last_a)
 
     def phase_back_flux_rims():
         for p in (0, 1, 14, 15):
@@ -510,8 +538,12 @@
 
     pl.semaphore_wait(barrier, 6)
     halo_a1 = start(
-        remote(av.at[:, last_a, :], xl_a, 0, to_right),
-        remote(av.at[:, 0, :], xr_a, 1, to_left),
+        remote(av.at[:, last_a, 0:128], xl_a.at[:, 0:128], 0, to_right),
+        remote(av.at[:, 0, 128:256], xr_a.at[:, 128:256], 1, to_left),
+    )
+    halo_a1_rest = start(
+        remote(av.at[:, last_a, 128:256], xl_a.at[:, 128:256], 32, to_right),
+        remote(av.at[:, 0, 0:128], xr_a.at[:, 0:128], 33, to_left),
     )
     loaded(mask_s, 0)
     loaded(sv_s, 1)
@@ -543,13 +575,19 @@
     wait(halo_y1)
     open_messages(from_lo, from_hi, halo_a, halo_o)
     phase_fix()
+    wait(halo_a1)
+    phase_air_ends()
+    phase_air_rims()
+    rim_a = start(
+        remote(rim_hi, S_a.at[0:8], 6, to_right),
+        remote(rim_lo, S_a.at[136:144], 7, to_left),
+    )
     wait(halo_o1)
     phase_sea_surface()
     rim_o = send_rims(S_o, S_o, 8)
-    wait(halo_a1)
+    wait(halo_a1_rest)
     phase_air_outer()
     phase_air_surface()
-    rim_a = send_rims(S_a, S_a, 6)
 
     loaded(st_s, 11)
     phase_forward_skin()
@@ -566,11 +604,12 @@
     phase_sea_columns()
     loaded(aw_s, 14)
     phase_air_forcing()
+    phase_air_pack()
+    wait(halo_o1_rest)
+    phase_sea_outer()
     wait(rim_a)
     wait(rim_o)
     phase_forward_rims()
-    wait(halo_o1_rest)
-    phase_sea_outer()
     phase_sea_columns_outer()
     halo_o2_rest = start(
         remote(adj.at[last_o, 8:64], xl2_o.at[8:64], 16, to_right),
@@ -583,7 +622,7 @@
         remote(Cf.at[0, 8:16], df_lo, 28, to_left_above),
         remote(Cf.at[2, 128:136], df_hi, 29, to_right_below),
     )
-    phase_air_pack()
+    phase_air_pack_outer()
     phase_own_outer()
     halo_a2 = start(remote(own_r, xl2_a, 18, to_right), remote(own_l, xr2_a, 19, to_left))
     phase_back_skin()
@@ -658,8 +697,8 @@
         dx, dx, ext, ext, V((128, 512), f32), V((128, 512), f32), blk, blk, blk, blk, cterm, cterm, blk, blk,
         rowa, rowa, rowo, rowo, pack, pack, pack, blk, pack, blk, blk, blk,
         rowa, rowa, rowo, rowo, pack, pack, pack, blk, pack,
-        rowa, rowa, V((8, sea_y), f32), V((8, sea_y), f32), blk, blk, tile, tile, tile, tile, tile, tile,
-        dma((15,)), dma((32,)), dma((32,)),
+        tile, tile, rowa, rowa, V((8, sea_y), f32), V((8, sea_y), f32), blk, blk, tile, tile, tile, tile, tile, tile,
+        dma((15,)), dma((34,)), dma((34,)),
     ]
     anywhere = pl.BlockSpec(memory_space=pl.ANY)
     outs = (jax.ShapeDtypeStruct(av.shape, f32), jax.ShapeDtypeStruct(sv.shape, f32))

time: 32.4 us -> 32.8 us (1.012)
  the two profiles are of different devices: /device:TPU:0 before, /device:TPU:7 now
where the time goes in v5:
time: 32.8 us; the launch traced here: 32.7 us
  Pallas kernels  32 us (98%)
  between operations  0.64 us (2%)
    pallas_call x1, Pallas kernels, shards(): pl.pallas_call(functools.partial(kernel, nx, ny, air_x, sea_x), out_shape...  30.4 us
    pallas_call x1, Pallas kernels, shards(): pl.pallas_call(deliver, out_shape=outs, in_specs=[anywhere] * 2, out_spec...  1.66 us

profile of v5, /device:TPU:7, one launch (start us, length us, event | category | flops | bytes accessed | tf_op | source)
XLA Modules:
  0.0 32.7 jit_solution(10327080242108239018)
XLA Ops:
  0.6 30.4 %shard_map.158 = (f32[16,128,256]{2,1,0:T(8,128)S(1)}, f32[8,64,512]{2,1,0:T(8,128)S(1)}) custom-call(f32[128,16,256]{2,1,0:T(8,128)} %av.1, f32[64,8,512]{2,1,0:T(8,128)} %sv.1, f32[128,16,256]{2,1,0:T(8,128)} %asc.1, f32[64,8,512]{2,1,0:T(8,128)} %ssc.1, f32[128,16,256]{2,1,0:T(8,128)} %aw.1, f32[64,8,512]{2,1,0:T(8,128)} %sw.1, f32[128,128]{1,0:T(8,128)} %wa.1, ...), custom_call_target="tpu_custom_call" | custom-call | flops 4000000000 | bytes 21000000 | tf_op jit(solution)/shard_map/pallas_call | solution.py:705
  31.0 1.7 %shard_map.159 = (f32[128,16,256]{2,1,0:T(8,128)}, f32[64,8,512]{2,1,0:T(8,128)}) custom-call(f32[16,128,256]{2,1,0:T(8,128)S(1)} %get-tuple-element.4.a, f32[8,64,512]{2,1,0:T(8,128)S(1)} %get-tuple-element.5.o), custom_call_target="tpu_custom_call" | custom-call | tf_op jit(solution)/shard_map/pallas_call | solution.py:716
